TPU v7x, 768 devices: a whole 4x8x12 slice. The times are simulated.
768 devices in a mesh: sx: 12 (over z_lo, x), sy: 32 (over z_hi, y), hb: 2 (over core).
Axes of the slice: x: 4, y: 8, z: 12 (z_hi: 4, z_lo: 3; z = z_hi * 3 + z_lo), core: 2. Of those that a mesh axis runs over, the one named last changes fastest.
Arguments:
- state: float32 [6, 5, 48, 256, 256], P('hb', None, 'sx', 'sy'), may hold values from -6 to 6
- forcing: float32 [6, 5, 48, 256, 256], P('hb', None, 'sx', 'sy'), may hold values from -6 to 6
- coef: float32 [48, 256, 256], P('sx', 'sy'), may hold values from 0.3 to 3
- mixing: float32 [5, 5], replicated, may hold values from -2.5 to 2.5
- agglomerate: int32 [48, 256, 256], P('sx', 'sy'), may hold values from 0 to 32767, as said below
Outputs:
- corrected: float32 [6, 5, 48, 256, 256], P('hb', None, 'sx', 'sy')
- residual: float32 [6, 5, 48, 256, 256], P('hb', None, 'sx', 'sy')
Inputs may be any that keep to these rules, and one draw needn't show every extreme that they name: `agglomerate`: A fine cell at global position (x, y, z) lies in coarse cell ((x mod 4) // 2, b, z // 2) of its group, with b = y // 2 where x is even, and otherwise b one of (y-1)//2, y//2, (y+1)//2 clipped to 0 .. 127; so every coarse cell holds four or more fine cells.
All inputs are finite; a program needn't handle non-finite values.
Results may differ from a plain program's by a relative error of at most 0.0001.
Values sent between devices are 32-bit elements; how exact they have to be, the bound alone decides.
No kernel may reach another device: no remote copies, remote signals or barrier semaphores. Data moves between devices by JAX's collectives and lax.ppermute only.
A program may use at most 128 MiB of HBM per device.

v0:
```python
import math

import jax
import jax.numpy as jnp
from jax import lax
from jax.sharding import PartitionSpec as P

INST = 6


def with_halo(array, sides, width):
    for axis, dim in sides:
        size, length = (lax.axis_size(axis), array.shape[dim])
        up = [(i, (i + 1) % size) for i in range(size - 1)]
        down = [(j, i) for i, j in up]
        last = lax.slice_in_dim(array, length - width, length, axis=dim)
        first = lax.slice_in_dim(array, 0, width, axis=dim)
        before = lax.ppermute(last, axis, up)
        after = lax.ppermute(first, axis, down)
        array = jnp.concatenate([before, array, after], axis=dim)
    return array


def spectral_matrix(number):
    rows = jnp.arange(number)[:, None]
    cols = jnp.arange(number)[None, :]
    diff = rows - cols
    same = diff == 0
    angle = jnp.where(same, 1.0, math.pi * diff.astype(jnp.float32) / number)
    signs = jnp.where(diff % 2 == 0, 1.0, -1.0)
    return jnp.where(same, 0.0, 0.5 * signs * jnp.cos(angle) / jnp.sin(angle))


def combine(field, padded, timed, cell_coef, mixing):
    deeper = jnp.pad(field, ((0, 0), (0, 0), (0, 0), (0, 0), (1, 1)))
    beside = padded[:, :, 2:, 1:-1, :] + padded[:, :, :-2, 1:-1, :]
    beside = beside + padded[:, :, 1:-1, 2:, :] + padded[:, :, 1:-1, :-2, :]
    beside = beside + deeper[:, :, :, :, 2:] + deeper[:, :, :, :, :-2]
    mixed = jnp.einsum("vw,iwxyz->ivxyz", mixing, field, precision=lax.Precision.HIGHEST)
    return cell_coef * (6.0 * field - beside) + mixed + timed + jnp.tanh(field)


def restrict_terms(values, selector):
    per_row = jnp.einsum("cxyz,rxyz->cxrz", values, selector, precision=lax.Precision.HIGHEST)
    number, size_x, window, size_z = per_row.shape
    return per_row.reshape(number, size_x // 2, 2, window, size_z // 2, 2).sum(axis=(2, 5))


def shards(state, forcing, coef, mixing, agglomerate):
    inst_here = state.shape[0]
    n_vars = state.shape[1]
    size_x, size_y, size_z = (state.shape[2], state.shape[3], state.shape[4])
    spectral = spectral_matrix(INST)
    spec_rows = lax.dynamic_slice_in_dim(spectral, lax.axis_index("hb") * inst_here, inst_here, 0)
    padded = with_halo(state, (("sx", 2), ("sy", 3)), 1)
    whole = lax.all_gather(state, "hb", axis=0, tiled=True)
    timed = jnp.einsum("ij,jvxyz->ivxyz", spec_rows, whole, precision=lax.Precision.HIGHEST)
    residual = forcing - combine(state, padded, timed, coef, mixing)
    coarse_x = size_x // 2
    own_rows = size_y // 2
    coarse_y = own_rows * lax.axis_size("sy")
    coarse_z = size_z // 2
    window = own_rows + 2
    first_row = lax.axis_index("sy") * own_rows - 1
    rows_local = agglomerate // coarse_z % coarse_y - first_row
    selector = (
        rows_local[None] == jnp.arange(window, dtype=jnp.int32)[:, None, None, None]
    ).astype(jnp.float32)
    fields_here = inst_here * n_vars
    stacked = jnp.concatenate(
        [
            residual.reshape(fields_here, size_x, size_y, size_z),
            state.reshape(fields_here, size_x, size_y, size_z),
            coef[None],
            jnp.ones((1, size_x, size_y, size_z), jnp.float32),
        ],
        axis=0,
    )
    terms = restrict_terms(stacked, selector)
    edges = jnp.concatenate([terms[:, :, :1], terms[:, :, -1:]], axis=2)
    rims = with_halo(edges, (("sy", 2),), 1)
    shares = terms[:, :, 1:-1]
    shares = shares.at[:, :, :1].add(rims[:, :, :1])
    shares = shares.at[:, :, -1:].add(rims[:, :, -1:])
    block = (inst_here, n_vars, coarse_x, own_rows, coarse_z)
    res_c = shares[:fields_here].reshape(block)
    sum_c = shares[fields_here : 2 * fields_here].reshape(block)
    coef_sum = shares[2 * fields_here]
    count = shares[2 * fields_here + 1]
    start = sum_c / count
    coef_c = coef_sum / count
    diagonal_term = 6.0 * coef_c + 2.0

    def coarse_apply(field):
        framed = with_halo(field, (("sx", 2), ("sy", 3)), 1)
        gathered = lax.all_gather(field, "hb", axis=0, tiled=True)
        coarse_timed = jnp.einsum(
            "ij,jvxyz->ivxyz", spec_rows, gathered, precision=lax.Precision.HIGHEST
        )
        return combine(field, framed, coarse_timed, coef_c, mixing)

    start_image = coarse_apply(start)
    target = start_image + res_c
    value = start + 0.6 * (target - start_image) / diagonal_term
    value = value + 0.6 * (target - coarse_apply(value)) / diagonal_term
    change = value - start
    margins = with_halo(change, (("sy", 3),), 1)
    widened = jnp.repeat(jnp.repeat(margins, 2, axis=2), 2, axis=4)
    fine_change = jnp.einsum(
        "ivxrz,rxyz->ivxyz", widened, selector, precision=lax.Precision.HIGHEST
    )
    corrected = state + fine_change
    return (corrected, residual)


def solution(mesh):
    return jax.shard_map(
        shards,
        mesh=mesh,
        in_specs=(
            P("hb", None, "sx", "sy", None),
            P("hb", None, "sx", "sy", None),
            P("sx", "sy", None),
            P(),
            P("sx", "sy", None),
        ),
        out_specs=(P("hb", None, "sx", "sy", None), P("hb", None, "sx", "sy", None)),
        check_vma=False,
    )
```

profile of v0, /device:TPU:646, one launch (start us, length us, event | category | flops | bytes accessed | tf_op | source)
XLA Modules:
  0.0 251.5 jit_solution(1686271439826515797)
XLA Ops:
  2.8 2.7 %collective-permute-start = (f32[3,5,1,8,256]{4,1,3,2,0:T(8,128)}, f32[3,5,1,8,256]{4,1,3,2,0:T(8,128)S(1)}, u32[]{:S(2)}, u32[]{:S(2)}) collective-permute-start(f32[3,5,1,8,256]{4,1,3,2,0:T(8,128)} %get-tuple-element.42), channel_id=1, source_target_pairs={{64,0},{128,64},{192,128},{256,192},{320,256},{384,320},{448,384},... | collective-permute-start | bytes 368648 | tf_op jit(solution)/shard_map/ppermute | solution.py:19
  5.6 5.2 %collective-permute-start.1 = (f32[3,5,1,8,256]{4,1,3,2,0:T(8,128)}, f32[3,5,1,8,256]{4,1,3,2,0:T(8,128)S(1)}, u32[]{:S(2)}, u32[]{:S(2)}) collective-permute-start(f32[3,5,1,8,256]{4,1,3,2,0:T(8,128)} %get-tuple-element.43), channel_id=1, source_target_pairs={{0,64},{64,128},{128,192},{192,256},{256,320},{320,384},{384,448},... | collective-permute-start | bytes 368648 | tf_op jit(solution)/shard_map/ppermute | solution.py:18
  10.8 2.7 %all_gather.9 = f32[6,5,4,8,256]{4,3,2,1,0:T(8,128)S(1)} all-gather(f32[3,5,4,8,256]{4,3,2,1,0:T(8,128)} %param.9), channel_id=1, replica_groups=mesh['sx'=12,'sy'=32,'hb'=2] {'hb'}, dimensions={0}, use_global_device_ids=true | all-gather | bytes 1474560 | tf_op jit(solution)/shard_map/all_gather | solution.py:56
  15.7 7.8 %collective-permute-start.2 = (f32[3,5,6,1,256]{4,1,3,2,0:T(8,128)S(1)}, f32[3,5,6,1,256]{4,1,3,2,0:T(8,128)S(1)}, u32[]{:S(2)}, u32[]{:S(2)}) collective-permute-start(f32[3,5,6,1,256]{4,1,3,2,0:T(8,128)S(1)} %get-tuple-element.38), channel_id=1, source_target_pairs={{2,0},{4,2},{6,4},{8,6},{10,8},{12,10},{14,12},{16,14},{18,16},{20... | collective-permute-start | bytes 276488 | tf_op jit(solution)/shard_map/ppermute | solution.py:19
  23.5 1.9 collective-permute-start.3
  26.9 13.4 %collective-permute-done.3 = f32[3,5,6,1,256]{4,1,3,2,0:T(8,128)} collective-permute-done((f32[3,5,6,1,256]{4,1,3,2,0:T(8,128)S(1)}, f32[3,5,6,1,256]{4,1,3,2,0:T(8,128)}, u32[]{:S(2)}, u32[]{:S(2)}) %collective-permute-start.3) | collective-permute-done | bytes 92192 | tf_op jit(solution)/shard_map/ppermute | solution.py:18
  40.3 3.8 %fusion.10 = f32[3,5,4,8,256]{4,1,3,2,0:T(8,128)S(1)} fusion(f32[3,5,4,8,256]{4,1,3,2,0:T(8,128)S(1)} %copy.129, f32[3,5,6,8,256]{4,1,3,2,0:T(8,128)} %copy-done.6, f32[3,5,6,1,256]{4,1,3,2,0:T(8,128)} %collective-permute-done.3, f32[3,5,6,1,256]{4,1,3,2,0:T(8,128)S(1)} %collective-permute-done.2, f32[3,5,1,8,256]{4,1,3,2,0:T(8,128)} %copy-done.8, ...), kind=kOutput, calls=%fused_computation.14 | convolution fusion | flops 9338880 | bytes 4470784 | tf_op jit(solution)/shard_map/vw,iwxyz->ivxyz/dot_general | solution.py:39
  45.1 2.8 %copy.143 = f32[32,4,8,256]{0,2,3,1:T(8,128)} copy(f32[32,4,8,256]{3,2,1,0:T(8,128)S(1)} %maximum_maximum_fusion) | data formatting | bytes 2097152 | tf_op jit(solution)/shard_map/concatenate | solution.py:70
  47.9 8.5 %fusion.1 = f32[4,256,6,32]{3,2,1,0:T(8,128)} fusion(f32[32,4,8,256]{0,2,3,1:T(8,128)} %copy.143, s32[4,8,256]{1,2,0:T(8,128)S(1)} %copy.128), kind=kOutput, calls=%fused_computation.3 | convolution fusion | flops 18923520 | bytes 1867776 | tf_op jit(solution)/shard_map/cxyz,rxyz->cxrz/dot_general | solution.py:44
  56.5 2.8 %reduce_sum.9 = f32[32,2,6,128]{0,2,3,1:T(8,128)S(1)} reduce(f32[32,2,2,6,128,2]{0,3,5,4,2,1:T(8,128)} %bitcast.87, f32[]{:T(128)} %constant.125.clone.1), dimensions={2,5}, to_apply=%region_0.1 | reduce | flops 147456 | bytes 983044 | tf_op jit(solution)/shard_map/reduce_sum | solution.py:46
  59.5 1.9 collective-permute-start.4
  61.5 9.3 %collective-permute-start.5 = (f32[32,2,1,128]{0,2,3,1:T(1,128)S(1)}, f32[32,2,1,128]{0,2,3,1:T(1,128)S(1)}, u32[]{:S(2)}, u32[]{:S(2)}) collective-permute-start(f32[32,2,1,128]{0,2,3,1:T(1,128)S(1)} %get-tuple-element.40), channel_id=1, source_target_pairs={{2,0},{4,2},{6,4},{8,6},{10,8},{12,10},{14,12},{16,14},{18,16},{20... | collective-permute-start | bytes 98312 | tf_op jit(solution)/shard_map/ppermute | solution.py:19
  72.1 3.2 %scatter-add.6 = f32[32,2,4,128]{0,2,3,1:T(4,128)S(1)} dynamic-update-slice(f32[32,2,4,128]{0,2,3,1:T(4,128)S(1)} %slice.233, f32[32,2,1,128]{0,2,3,1:T(1,128)S(1)} %slice_add_fusion.1, s32[]{:T(128)} %constant.116.clone.1, s32[]{:T(128)} %constant.116.clone.1, s32[]{:T(128)} %constant.116.clone.1, s32[]{:T(128)} %constant.116.clone.1) | dynamic-update-slice | bytes 65540 | tf_op jit(solution)/shard_map/scatter-add | solution.py:83
  75.5 3.2 %scatter-add.9 = f32[32,2,4,128]{0,2,3,1:T(4,128)S(1)} dynamic-update-slice(f32[32,2,4,128]{0,2,3,1:T(4,128)S(1)} %scatter-add.6, f32[32,2,1,128]{0,2,3,1:T(1,128)S(1)} %slice_add_fusion, s32[]{:T(128)} %constant.116.clone.1, s32[]{:T(128)} %constant.116.clone.1, s32[]{:T(128)} %constant.131.clone.1, s32[]{:T(128)} %constant.116.clone.1) | dynamic-update-slice | bytes 65540 | tf_op jit(solution)/shard_map/scatter-add | solution.py:84
  82.0 3.2 %collective-permute-start.7 = (f32[3,5,1,4,128]{4,1,3,2,0:T(8,128)S(1)}, f32[3,5,1,4,128]{4,1,3,2,0:T(8,128)S(1)}, u32[]{:S(2)}, u32[]{:S(2)}) collective-permute-start(f32[3,5,1,4,128]{4,1,3,2,0:T(8,128)S(1)} %get-tuple-element.56), channel_id=1, source_target_pairs={{0,64},{64,128},{128,192},{192,256},{256,320},{320,384},{384,448},... | collective-permute-start | bytes 92168 | tf_op jit(solution)/shard_map/ppermute | solution.py:18
  85.3 2.6 %collective-permute-start.6 = (f32[3,5,1,4,128]{4,1,3,2,0:T(8,128)S(1)}, f32[3,5,1,4,128]{4,1,3,2,0:T(8,128)S(1)}, u32[]{:S(2)}, u32[]{:S(2)}) collective-permute-start(f32[3,5,1,4,128]{4,1,3,2,0:T(8,128)S(1)} %get-tuple-element.57), channel_id=1, source_target_pairs={{64,0},{128,64},{192,128},{256,192},{320,256},{384,320},{448,384},... | collective-permute-start | bytes 92168 | tf_op jit(solution)/shard_map/ppermute | solution.py:19
  88.4 5.0 %collective-permute-done.6 = f32[3,5,1,4,128]{4,1,3,2,0:T(8,128)S(1)} collective-permute-done((f32[3,5,1,4,128]{4,1,3,2,0:T(8,128)S(1)}, f32[3,5,1,4,128]{4,1,3,2,0:T(8,128)S(1)}, u32[]{:S(2)}, u32[]{:S(2)}) %collective-permute-start.6) | collective-permute-done | bytes 30752 | tf_op jit(solution)/shard_map/ppermute | solution.py:19
  93.4 8.5 %collective-permute-start.8 = (f32[3,5,4,1,128]{4,1,3,2,0:T(8,128)S(1)}, f32[3,5,4,1,128]{4,1,3,2,0:T(8,128)S(1)}, u32[]{:S(2)}, u32[]{:S(2)}) collective-permute-start(f32[3,5,4,1,128]{4,1,3,2,0:T(8,128)S(1)} %get-tuple-element.50), channel_id=1, source_target_pairs={{2,0},{4,2},{6,4},{8,6},{10,8},{12,10},{14,12},{16,14},{18,16},{20... | collective-permute-start | bytes 92168 | tf_op jit(solution)/shard_map/ppermute | solution.py:19
  101.9 1.9 collective-permute-start.9
  104.0 9.0 %collective-permute-done.9 = f32[3,5,4,1,128]{4,1,3,2,0:T(8,128)S(1)} collective-permute-done((f32[3,5,4,1,128]{4,1,3,2,0:T(8,128)S(1)}, f32[3,5,4,1,128]{4,1,3,2,0:T(8,128)S(1)}, u32[]{:S(2)}, u32[]{:S(2)}) %collective-permute-start.9) | collective-permute-done | bytes 30752 | tf_op jit(solution)/shard_map/ppermute | solution.py:18
  113.3 1.9 collective-permute-start.11
  115.2 3.9 %collective-permute-start.10 = (f32[3,5,1,4,128]{4,1,3,2,0:T(8,128)S(1)}, f32[3,5,1,4,128]{4,1,3,2,0:T(8,128)S(1)}, u32[]{:S(2)}, u32[]{:S(2)}) collective-permute-start(f32[3,5,1,4,128]{4,1,3,2,0:T(8,128)S(1)} %get-tuple-element.55), channel_id=1, source_target_pairs={{64,0},{128,64},{192,128},{256,192},{320,256},{384,320},{448,384},... | collective-permute-start | bytes 92168 | tf_op jit(solution)/shard_map/ppermute | solution.py:19
  121.1 2.3 collective-permute-done.10
  123.3 2.8 %collective-permute-start.12 = (f32[3,5,4,1,128]{4,1,3,2,0:T(8,128)S(1)}, f32[3,5,4,1,128]{4,1,3,2,0:T(8,128)S(1)}, u32[]{:S(2)}, u32[]{:S(2)}) collective-permute-start(f32[3,5,4,1,128]{4,1,3,2,0:T(8,128)S(1)} %get-tuple-element.48), channel_id=1, source_target_pairs={{2,0},{4,2},{6,4},{8,6},{10,8},{12,10},{14,12},{16,14},{18,16},{20... | collective-permute-start | bytes 92168 | tf_op jit(solution)/shard_map/ppermute | solution.py:19
  126.2 3.0 %collective-permute-start.13 = (f32[3,5,4,1,128]{4,1,3,2,0:T(8,128)S(1)}, f32[3,5,4,1,128]{4,1,3,2,0:T(8,128)S(1)}, u32[]{:S(2)}, u32[]{:S(2)}) collective-permute-start(f32[3,5,4,1,128]{4,1,3,2,0:T(8,128)S(1)} %get-tuple-element.49), channel_id=1, source_target_pairs={{0,2},{2,4},{4,6},{6,8},{8,10},{10,12},{12,14},{14,16},{16,18},{18... | collective-permute-start | bytes 92168 | tf_op jit(solution)/shard_map/ppermute | solution.py:18
  129.5 7.9 %collective-permute-done.13 = f32[3,5,4,1,128]{4,1,3,2,0:T(8,128)S(1)} collective-permute-done((f32[3,5,4,1,128]{4,1,3,2,0:T(8,128)S(1)}, f32[3,5,4,1,128]{4,1,3,2,0:T(8,128)S(1)}, u32[]{:S(2)}, u32[]{:S(2)}) %collective-permute-start.13) | collective-permute-done | bytes 30752 | tf_op jit(solution)/shard_map/ppermute | solution.py:18
  137.8 1.9 collective-permute-start.14
  139.7 9.0 %collective-permute-start.15 = (f32[3,5,2,1,128]{4,1,3,2,0:T(8,128)S(1)}, f32[3,5,2,1,128]{4,1,3,2,0:T(8,128)S(1)}, u32[]{:S(2)}, u32[]{:S(2)}) collective-permute-start(f32[3,5,2,1,128]{4,1,3,2,0:T(8,128)S(1)} %get-tuple-element.53), channel_id=1, source_target_pairs={{2,0},{4,2},{6,4},{8,6},{10,8},{12,10},{14,12},{16,14},{18,16},{20... | collective-permute-start | bytes 46088 | tf_op jit(solution)/shard_map/ppermute | solution.py:19
  148.7 7.4 %copy.157 = f32[3,5,4,8,256]{1,3,0,4,2:T(8,128)} copy(f32[3,5,4,8,256]{4,3,2,1,0:T(8,128)S(1)} %copy-done.2) | data formatting | bytes 983040 | tf_op args[0]
  157.7 5.3 %broadcast_in_dim.40 = f32[3,5,4,6,128,2]{3,1,0,5,4,2:T(8,128)} broadcast(f32[3,5,4,6,128]{3,1,0,4,2:T(8,128)S(1)} %bitcast.86), dimensions={0,1,2,3,4} | broadcast | bytes 552960 | tf_op jit(solution)/shard_map/broadcast_in_dim | solution.py:108
  163.0 80.0 %bitcast_add_fusion = f32[3,5,4,8,256]{1,3,0,4,2:T(8,128)} fusion(f32[3,5,4,8,256]{1,3,0,4,2:T(8,128)} %copy.157, f32[3,5,4,6,256]{3,1,0,4,2:T(8,128)} %bitcast.85, s32[4,8,256]{1,2,0:T(8,128)S(1)} %copy-done.4), kind=kOutput, calls=%fused_computation | convolution fusion | flops 9019392 | bytes 1384448 | tf_op jit(solution)/shard_map/ivxrz,rxyz->ivxyz/dot_general | solution.py:109
  243.0 8.4 %copy.158 = f32[3,5,4,8,256]{4,3,2,1,0:T(8,128)} copy(f32[3,5,4,8,256]{1,3,0,4,2:T(8,128)} %bitcast_add_fusion) | data formatting | bytes 983040
  (74 shorter events, 16.9 us)
Async XLA Ops:
  0.6 39.6 %copy-start = (f32[5,5]{1,0:T(8,128)S(1)}, f32[5,5]{1,0:T(8,128)}, u32[]{:S(2)}) copy-start(f32[5,5]{1,0:T(8,128)} %param.12) | copy-start | bytes 304
  0.6 14.7 %copy-start.2 = (f32[3,5,4,8,256]{4,3,2,1,0:T(8,128)S(1)}, f32[3,5,4,8,256]{4,3,2,1,0:T(8,128)}, u32[]{:S(2)}) copy-start(f32[3,5,4,8,256]{4,3,2,1,0:T(8,128)} %param.9) | copy-start | bytes 1474564
  0.7 24.8 %copy-start.10 = (s32[4,8,256]{2,1,0:T(8,128)S(1)}, s32[4,8,256]{2,1,0:T(8,128)}, u32[]{:S(2)}) copy-start(s32[4,8,256]{2,1,0:T(8,128)} %param.13) | copy-start | bytes 98308
  0.7 39.6 %copy-start.9 = (f32[4,8,256]{2,1,0:T(8,128)S(1)}, f32[4,8,256]{2,1,0:T(8,128)}, u32[]{:S(2)}) copy-start(f32[4,8,256]{2,1,0:T(8,128)} %param.11) | copy-start | bytes 98308
  2.8 12.8 %collective-permute-start = (f32[3,5,1,8,256]{4,1,3,2,0:T(8,128)}, f32[3,5,1,8,256]{4,1,3,2,0:T(8,128)S(1)}, u32[]{:S(2)}, u32[]{:S(2)}) collective-permute-start(f32[3,5,1,8,256]{4,1,3,2,0:T(8,128)} %get-tuple-element.42), channel_id=1, source_target_pairs={{64,0},{128,64},{192,128},{256,192},{320,256},{384,320},{448,384},... | collective-permute-start | bytes 368648 | tf_op jit(solution)/shard_map/ppermute | solution.py:19
  5.6 9.7 %collective-permute-start.1 = (f32[3,5,1,8,256]{4,1,3,2,0:T(8,128)}, f32[3,5,1,8,256]{4,1,3,2,0:T(8,128)S(1)}, u32[]{:S(2)}, u32[]{:S(2)}) collective-permute-start(f32[3,5,1,8,256]{4,1,3,2,0:T(8,128)} %get-tuple-element.43), channel_id=1, source_target_pairs={{0,64},{64,128},{128,192},{192,256},{256,320},{320,384},{384,448},... | collective-permute-start | bytes 368648 | tf_op jit(solution)/shard_map/ppermute | solution.py:18
  15.3 10.1 %copy-start.8 = (f32[3,5,1,8,256]{4,1,3,2,0:T(8,128)}, f32[3,5,1,8,256]{4,1,3,2,0:T(8,128)S(1)}, u32[]{:S(2)}) copy-start(f32[3,5,1,8,256]{4,1,3,2,0:T(8,128)S(1)} %collective-permute-done.1) | copy-start | bytes 368644
  15.7 9.8 %copy-start.7 = (f32[3,5,1,8,256]{4,1,3,2,0:T(8,128)}, f32[3,5,1,8,256]{4,1,3,2,0:T(8,128)S(1)}, u32[]{:S(2)}) copy-start(f32[3,5,1,8,256]{4,1,3,2,0:T(8,128)S(1)} %collective-permute-done) | copy-start | bytes 368644
  15.7 9.8 %copy-start.6 = (f32[3,5,6,8,256]{4,1,3,2,0:T(8,128)}, f32[3,5,6,8,256]{4,1,3,2,0:T(8,128)S(1)}, u32[]{:S(2)}) copy-start(f32[3,5,6,8,256]{4,1,3,2,0:T(8,128)S(1)} %constant_dynamic-update-slice_fusion) | copy-start | bytes 2211844
  15.7 11.2 %collective-permute-start.2 = (f32[3,5,6,1,256]{4,1,3,2,0:T(8,128)S(1)}, f32[3,5,6,1,256]{4,1,3,2,0:T(8,128)S(1)}, u32[]{:S(2)}, u32[]{:S(2)}) collective-permute-start(f32[3,5,6,1,256]{4,1,3,2,0:T(8,128)S(1)} %get-tuple-element.38), channel_id=1, source_target_pairs={{2,0},{4,2},{6,4},{8,6},{10,8},{12,10},{14,12},{16,14},{18,16},{20... | collective-permute-start | bytes 276488 | tf_op jit(solution)/shard_map/ppermute | solution.py:19
  23.5 16.8 %collective-permute-start.3 = (f32[3,5,6,1,256]{4,1,3,2,0:T(8,128)S(1)}, f32[3,5,6,1,256]{4,1,3,2,0:T(8,128)}, u32[]{:S(2)}, u32[]{:S(2)}) collective-permute-start(f32[3,5,6,1,256]{4,1,3,2,0:T(8,128)S(1)} %get-tuple-element.39), channel_id=1, source_target_pairs={{0,2},{2,4},{4,6},{6,8},{8,10},{10,12},{12,14},{14,16},{16,18},{18... | collective-permute-start | bytes 276488 | tf_op jit(solution)/shard_map/ppermute | solution.py:18
  25.7 22.2 %copy-start.3 = (s32[4,8,256]{1,2,0:T(8,128)}, s32[4,8,256]{1,2,0:T(8,128)S(1)}, u32[]{:S(2)}) copy-start(s32[4,8,256]{1,2,0:T(8,128)S(1)} %copy.128) | copy-start | bytes 98308
  44.2 0.8 copy-start.5
  59.5 12.4 %collective-permute-start.4 = (f32[32,2,1,128]{0,2,3,1:T(1,128)S(1)}, f32[32,2,1,128]{0,2,3,1:T(1,128)S(1)}, u32[]{:S(2)}, u32[]{:S(2)}) collective-permute-start(f32[32,2,1,128]{0,2,3,1:T(1,128)S(1)} %get-tuple-element.41), channel_id=1, source_target_pairs={{0,2},{2,4},{4,6},{6,8},{8,10},{10,12},{12,14},{14,16},{16,18},{18... | collective-permute-start | bytes 98312 | tf_op jit(solution)/shard_map/ppermute | solution.py:18
  61.5 13.8 %collective-permute-start.5 = (f32[32,2,1,128]{0,2,3,1:T(1,128)S(1)}, f32[32,2,1,128]{0,2,3,1:T(1,128)S(1)}, u32[]{:S(2)}, u32[]{:S(2)}) collective-permute-start(f32[32,2,1,128]{0,2,3,1:T(1,128)S(1)} %get-tuple-element.40), channel_id=1, source_target_pairs={{2,0},{4,2},{6,4},{8,6},{10,8},{12,10},{14,12},{16,14},{18,16},{20... | collective-permute-start | bytes 98312 | tf_op jit(solution)/shard_map/ppermute | solution.py:19
  82.0 6.3 %collective-permute-start.7 = (f32[3,5,1,4,128]{4,1,3,2,0:T(8,128)S(1)}, f32[3,5,1,4,128]{4,1,3,2,0:T(8,128)S(1)}, u32[]{:S(2)}, u32[]{:S(2)}) collective-permute-start(f32[3,5,1,4,128]{4,1,3,2,0:T(8,128)S(1)} %get-tuple-element.56), channel_id=1, source_target_pairs={{0,64},{64,128},{128,192},{192,256},{256,320},{320,384},{384,448},... | collective-permute-start | bytes 92168 | tf_op jit(solution)/shard_map/ppermute | solution.py:18
  85.3 8.1 %collective-permute-start.6 = (f32[3,5,1,4,128]{4,1,3,2,0:T(8,128)S(1)}, f32[3,5,1,4,128]{4,1,3,2,0:T(8,128)S(1)}, u32[]{:S(2)}, u32[]{:S(2)}) collective-permute-start(f32[3,5,1,4,128]{4,1,3,2,0:T(8,128)S(1)} %get-tuple-element.57), channel_id=1, source_target_pairs={{64,0},{128,64},{192,128},{256,192},{320,256},{384,320},{448,384},... | collective-permute-start | bytes 92168 | tf_op jit(solution)/shard_map/ppermute | solution.py:19
  93.4 10.6 %collective-permute-start.8 = (f32[3,5,4,1,128]{4,1,3,2,0:T(8,128)S(1)}, f32[3,5,4,1,128]{4,1,3,2,0:T(8,128)S(1)}, u32[]{:S(2)}, u32[]{:S(2)}) collective-permute-start(f32[3,5,4,1,128]{4,1,3,2,0:T(8,128)S(1)} %get-tuple-element.50), channel_id=1, source_target_pairs={{2,0},{4,2},{6,4},{8,6},{10,8},{12,10},{14,12},{16,14},{18,16},{20... | collective-permute-start | bytes 92168 | tf_op jit(solution)/shard_map/ppermute | solution.py:19
  101.9 11.1 %collective-permute-start.9 = (f32[3,5,4,1,128]{4,1,3,2,0:T(8,128)S(1)}, f32[3,5,4,1,128]{4,1,3,2,0:T(8,128)S(1)}, u32[]{:S(2)}, u32[]{:S(2)}) collective-permute-start(f32[3,5,4,1,128]{4,1,3,2,0:T(8,128)S(1)} %get-tuple-element.51), channel_id=1, source_target_pairs={{0,2},{2,4},{4,6},{6,8},{8,10},{10,12},{12,14},{14,16},{16,18},{18... | collective-permute-start | bytes 92168 | tf_op jit(solution)/shard_map/ppermute | solution.py:18
  113.3 7.8 %collective-permute-start.11 = (f32[3,5,1,4,128]{4,1,3,2,0:T(8,128)S(1)}, f32[3,5,1,4,128]{4,1,3,2,0:T(8,128)S(1)}, u32[]{:S(2)}, u32[]{:S(2)}) collective-permute-start(f32[3,5,1,4,128]{4,1,3,2,0:T(8,128)S(1)} %get-tuple-element.54), channel_id=1, source_target_pairs={{0,64},{64,128},{128,192},{192,256},{256,320},{320,384},{384,448},... | collective-permute-start | bytes 92168 | tf_op jit(solution)/shard_map/ppermute | solution.py:18
  115.2 8.1 %collective-permute-start.10 = (f32[3,5,1,4,128]{4,1,3,2,0:T(8,128)S(1)}, f32[3,5,1,4,128]{4,1,3,2,0:T(8,128)S(1)}, u32[]{:S(2)}, u32[]{:S(2)}) collective-permute-start(f32[3,5,1,4,128]{4,1,3,2,0:T(8,128)S(1)} %get-tuple-element.55), channel_id=1, source_target_pairs={{64,0},{128,64},{192,128},{256,192},{320,256},{384,320},{448,384},... | collective-permute-start | bytes 92168 | tf_op jit(solution)/shard_map/ppermute | solution.py:19
  123.3 6.1 %collective-permute-start.12 = (f32[3,5,4,1,128]{4,1,3,2,0:T(8,128)S(1)}, f32[3,5,4,1,128]{4,1,3,2,0:T(8,128)S(1)}, u32[]{:S(2)}, u32[]{:S(2)}) collective-permute-start(f32[3,5,4,1,128]{4,1,3,2,0:T(8,128)S(1)} %get-tuple-element.48), channel_id=1, source_target_pairs={{2,0},{4,2},{6,4},{8,6},{10,8},{12,10},{14,12},{16,14},{18,16},{20... | collective-permute-start | bytes 92168 | tf_op jit(solution)/shard_map/ppermute | solution.py:19
  126.2 11.3 %collective-permute-start.13 = (f32[3,5,4,1,128]{4,1,3,2,0:T(8,128)S(1)}, f32[3,5,4,1,128]{4,1,3,2,0:T(8,128)S(1)}, u32[]{:S(2)}, u32[]{:S(2)}) collective-permute-start(f32[3,5,4,1,128]{4,1,3,2,0:T(8,128)S(1)} %get-tuple-element.49), channel_id=1, source_target_pairs={{0,2},{2,4},{4,6},{6,8},{8,10},{10,12},{12,14},{14,16},{16,18},{18... | collective-permute-start | bytes 92168 | tf_op jit(solution)/shard_map/ppermute | solution.py:18
  137.8 18.3 %collective-permute-start.14 = (f32[3,5,2,1,128]{4,1,3,2,0:T(8,128)S(1)}, f32[3,5,2,1,128]{4,1,3,2,0:T(8,128)S(1)}, u32[]{:S(2)}, u32[]{:S(2)}) collective-permute-start(f32[3,5,2,1,128]{4,1,3,2,0:T(8,128)S(1)} %get-tuple-element.52), channel_id=1, source_target_pairs={{0,2},{2,4},{4,6},{6,8},{8,10},{10,12},{12,14},{14,16},{16,18},{18... | collective-permute-start | bytes 46088 | tf_op jit(solution)/shard_map/ppermute | solution.py:18
  139.7 16.4 %collective-permute-start.15 = (f32[3,5,2,1,128]{4,1,3,2,0:T(8,128)S(1)}, f32[3,5,2,1,128]{4,1,3,2,0:T(8,128)S(1)}, u32[]{:S(2)}, u32[]{:S(2)}) collective-permute-start(f32[3,5,2,1,128]{4,1,3,2,0:T(8,128)S(1)} %get-tuple-element.53), channel_id=1, source_target_pairs={{2,0},{4,2},{6,4},{8,6},{10,8},{12,10},{14,12},{16,14},{18,16},{20... | collective-permute-start | bytes 46088 | tf_op jit(solution)/shard_map/ppermute | solution.py:19
  157.7 5.3 %copy-start.4 = (s32[4,8,256]{1,2,0:T(8,128)S(1)}, s32[4,8,256]{1,2,0:T(8,128)}, u32[]{:S(2)}) copy-start(s32[4,8,256]{1,2,0:T(8,128)} %copy-done.3) | copy-start | bytes 98308
  163.0 88.3 %copy-start.1 = (f32[5,5]{1,0:T(8,128)S(1)}, f32[5,5]{1,0:T(8,128)}, u32[]{:S(2)}) copy-start(f32[5,5]{1,0:T(8,128)} %param.12) | copy-start | bytes 304
where the time goes:
time: 253 us; the launch traced here: 252 us
  matrix products  95.1 us (38%)
  starting transfers between devices  67.7 us (27%)
  waiting for transfers between devices  39.7 us (16%)
  local copies, waits for them, and re-layouts  37.6 us (15%)
  blocking collectives  6.51 us (3%)
  other arithmetic  3.49 us (1%)
    dot_general x1, matrix products, shards(): jnp.einsum('ivxrz,rxyz->ivxyz', widened, selector, precision=lax.Precisio...  80 us
    ppermute x8, starting transfers between devices, with_halo(): after = lax.ppermute(first, axis, down)  46.7 us
    ppermute x8, waiting for transfers between devices, with_halo(): before = lax.ppermute(last, axis, up)  31.3 us
    ppermute x8, starting transfers between devices, with_halo(): before = lax.ppermute(last, axis, up)  21.1 us
    unnamed x27, local copies, waits for them, and re-layouts  18.2 us
    dot_general x1, matrix products, restrict_terms(): jnp.einsum('cxyz,rxyz->cxrz', values, selector, precision=lax.Precision.H...  8.55 us
    ppermute x8, waiting for transfers between devices, with_halo(): after = lax.ppermute(first, axis, down)  8.35 us
    broadcast_in_dim x2, local copies, waits for them, and re-layouts, shards(): widened = jnp.repeat(jnp.repeat(margins, 2, axis=2), 2, axis=4)  5.72 us
  transfers between devices with their start and end apart: 16, of which 7 were waited for; matrix products, arithmetic and copies ran while one was open for 6% of the time, Pallas kernels for 0%

commit v1 on v0

v1 whole, which is shorter than its diff:
```python
import functools

import jax
import jax.numpy as jnp
import numpy as np
from jax import lax
from jax.experimental import pallas as pl
from jax.experimental.pallas import tpu as pltpu
from jax.sharding import PartitionSpec as P

INST = 6
HERE = 3
VARS = 5
FIELDS = HERE * VARS
PLANES = 4
ROWS = 8
NZ = 256
CZ = 128
GROUP = 16
WIN = 2 * GROUP
F32 = jnp.float32
BF16 = jnp.bfloat16


def spectral_matrix():
    rows = np.arange(INST)[:, None]
    cols = np.arange(INST)[None, :]
    diff = rows - cols
    same = diff == 0
    angle = np.where(same, 1.0, np.pi * diff / INST).astype(np.float32)
    signs = np.where(diff % 2 == 0, 1.0, -1.0).astype(np.float32)
    return np.where(same, 0.0, 0.5 * signs * np.cos(angle) / np.sin(angle))


SPECTRAL = spectral_matrix()
OWN = [[float(SPECTRAL[i, j]) for j in range(HERE)] for i in range(HERE)]
OTHER = [[float(SPECTRAL[i, j + HERE]) for j in range(HERE)] for i in range(HERE)]


def tile(field, plane):
    return pl.ds((field * PLANES + plane) * ROWS, ROWS)


def window(plane, field):
    return pl.ds((plane * GROUP + field) * ROWS, ROWS)


def row_of(index):
    return pl.ds(index, WIN, stride=ROWS)


def iota(shape, dim):
    return lax.broadcasted_iota(jnp.int32, shape, dim)


def moved_mask(agg_ref, plane):
    block = agg_ref[pl.ds((2 * plane + 1) * ROWS, ROWS), :]
    own = iota((ROWS, NZ), 0) >> 1
    return (((block >> 7) ^ own) & 1).astype(F32)


def pair_sums(values, ones):
    high = values.astype(BF16)
    low = (values - high.astype(F32)).astype(BF16)
    return jnp.dot(high, ones, preferred_element_type=F32) + jnp.dot(
        low, ones, preferred_element_type=F32
    )


def shift_rows(value, amount):
    return pltpu.roll(value, amount % value.shape[0], 0)


def shift_lanes(value, amount):
    return pltpu.roll(value, amount % value.shape[1], 1)


def edges_kernel(state, x_up, x_down, y_up, y_down, halves):
    for field in range(FIELDS):
        x_up[pl.ds(field * ROWS, ROWS), :] = state[tile(field, PLANES - 1), :]
        x_down[pl.ds(field * ROWS, ROWS), :] = state[tile(field, 0), :]
    count = FIELDS * PLANES
    for half in range(2):
        lanes = pl.ds(half * 128, 128)
        halves[half] = state[:, lanes]
        y_up[:, lanes] = halves[half, pl.ds(ROWS - 1, count, stride=ROWS), :]
        y_down[:, lanes] = halves[half, pl.ds(0, count, stride=ROWS), :]


def split_moved(even, odd, mask, parity, inside):
    moved = odd * mask
    beside = jnp.where(parity, shift_rows(moved, -1), shift_rows(moved, 1))
    return even + (odd - moved) + jnp.where(inside, beside, 0.0), beside


def fill_windows(out, sums, rims, summed, ones):
    summed[pl.ds(0, WIN * ROWS), :] = pair_sums(sums[...], ones)
    first = jnp.concatenate([rims[h, row_of(0), :] for h in range(2)], axis=1)
    last = jnp.concatenate([rims[h, row_of(ROWS - 1), :] for h in range(2)], axis=1)
    rim = pair_sums(jnp.concatenate([first, last], axis=0), ones)
    nothing = jnp.zeros((WIN, CZ), F32)
    out[row_of(0), :] = nothing
    out[row_of(7), :] = nothing
    out[row_of(1), :] = rim[WIN:]
    out[row_of(6), :] = rim[:WIN]
    for b in range(4):
        out[row_of(b + 2), :] = summed[row_of(2 * b), :] + summed[row_of(2 * b + 1), :]


def pair_matrix():
    return (iota((NZ, CZ), 0) >> 1 == iota((NZ, CZ), 1)).astype(BF16)


def inner_kernel(mixing, state, forcing, coef, agg, partial, s_win, sums, rims, summed):
    lane = iota((ROWS, NZ), 1)
    row = iota((ROWS, NZ), 0)
    mix = [[mixing[v, w] for w in range(VARS)] for v in range(VARS)]
    for x in range(PLANES):
        c = coef[pl.ds(x * ROWS, ROWS), :]
        for i in range(HERE):
            values = [state[tile(i * VARS + v, x), :] for v in range(VARS)]
            for v in range(VARS):
                field = i * VARS + v
                here = values[v]
                beside = jnp.where(lane == NZ - 1, 0.0, shift_lanes(here, -1))
                beside = beside + jnp.where(lane == 0, 0.0, shift_lanes(here, 1))
                beside = beside + jnp.where(row == ROWS - 1, 0.0, shift_rows(here, -1))
                beside = beside + jnp.where(row == 0, 0.0, shift_rows(here, 1))
                if x > 0:
                    beside = beside + state[tile(field, x - 1), :]
                if x < PLANES - 1:
                    beside = beside + state[tile(field, x + 1), :]
                total = c * (6.0 * here - beside) + jnp.tanh(here)
                for w in range(VARS):
                    total = total + mix[v][w] * values[w]
                for j in range(HERE):
                    if j != i:
                        total = total + OWN[i][j] * state[tile(j * VARS + v, x), :]
                partial[tile(field, x), :] = forcing[tile(field, x), :] - total
    ones = pair_matrix()
    parity = row % 2 == 1
    inside = (row > 0) & (row < ROWS - 1)
    for p in range(2):
        mask = moved_mask(agg, p)
        for field in range(GROUP):
            if field < FIELDS:
                even, odd = (state[tile(field, 2 * p), :], state[tile(field, 2 * p + 1), :])
            else:
                even = coef[pl.ds(2 * p * ROWS, ROWS), :]
                odd = coef[pl.ds((2 * p + 1) * ROWS, ROWS), :]
            kept, beside = split_moved(even, odd, mask, parity, inside)
            sums[window(p, field), :] = kept
            for half in range(2):
                rims[half, window(p, field), :] = beside[:, half * 128 : (half + 1) * 128]
    fill_windows(s_win, sums, rims, summed, ones)


def damping(coef_sum, count):
    inverse = jnp.where(count > 0.0, 1.0 / jnp.maximum(count, 1.0), 0.0)
    coef_c = coef_sum * inverse
    return inverse, coef_c, 0.6 / (6.0 * coef_c + 2.0)


def outer_kernel(
    partial, x_lo, x_hi, y_lo, y_hi, other, coef, agg, s_win,
    residual, r_win, up, down, sums, rims, summed, edge, scaled, halves, coefs,
):
    row = iota((ROWS, NZ), 0)
    for x in range(PLANES):
        c = coef[pl.ds(x * ROWS, ROWS), :]
        for i in range(HERE):
            for v in range(VARS):
                field = i * VARS + v
                total = partial[tile(field, x), :]
                for j in range(HERE):
                    total = total - OTHER[i][j] * other[tile(j * VARS + v, x), :]
                if x == 0:
                    total = total + c * x_lo[pl.ds(field * ROWS, ROWS), :]
                if x == PLANES - 1:
                    total = total + c * x_hi[pl.ds(field * ROWS, ROWS), :]
                for half in range(2):
                    halves[half, tile(field, x), :] = total[:, half * 128 : (half + 1) * 128]
    count = FIELDS * PLANES
    for half in range(2):
        lanes = pl.ds(half * 128, 128)
        coefs[half] = coef[:, lanes]
        for y, halo in ((0, y_lo), (ROWS - 1, y_hi)):
            c4 = coefs[half, pl.ds(y, PLANES, stride=ROWS), :]
            edge[pl.ds(0, PLANES), :] = c4
            edge[pl.ds(PLANES, PLANES), :] = c4
            c8 = edge[...]
            c60 = jnp.concatenate([c8] * (count // 8) + [c8[: count % 8]], axis=0)
            rows = pl.ds(y, count, stride=ROWS)
            halves[half, rows, :] = halves[half, rows, :] + c60 * halo[:, lanes]
        residual[:, lanes] = halves[half]
    ones = pair_matrix()
    parity = row % 2 == 1
    inside = (row > 0) & (row < ROWS - 1)
    for p in range(2):
        mask = moved_mask(agg, p)
        for field in range(GROUP):
            if field < FIELDS:
                even, odd = (residual[tile(field, 2 * p), :], residual[tile(field, 2 * p + 1), :])
            else:
                even = odd = jnp.ones((ROWS, NZ), F32)
            kept, beside = split_moved(even, odd, mask, parity, inside)
            sums[window(p, field), :] = kept
            for half in range(2):
                rims[half, window(p, field), :] = beside[:, half * 128 : (half + 1) * 128]
    fill_windows(r_win, sums, rims, summed, ones)
    for p in range(2):
        _, _, scale = damping(s_win[window(p, FIELDS), :], r_win[window(p, FIELDS), :])
        for field in range(GROUP):
            scaled[window(p, field), :] = scale * r_win[window(p, field), :]
    for out, ready, edge_row, rim_row in ((up, 4, 5, 6), (down, 3, 2, 1)):
        out[pl.ds(0, WIN), :] = scaled[row_of(ready), :]
        out[pl.ds(WIN, WIN), :] = r_win[row_of(edge_row), :]
        out[pl.ds(2 * WIN, WIN), :] = r_win[row_of(rim_row), :]
        out[pl.ds(3 * WIN, WIN), :] = s_win[row_of(edge_row), :]
        out[pl.ds(4 * WIN, WIN), :] = s_win[row_of(rim_row), :]


def first_kernel(r_in, s_in, lo, hi, r_out, s_out, delta, low_plane, high_plane):
    r_out[...] = r_in[...]
    s_out[...] = s_in[...]
    for msg, edge_row, rim_row in ((lo, 1, 2), (hi, 6, 5)):
        r_out[row_of(edge_row), :] = r_out[row_of(edge_row), :] + msg[pl.ds(WIN, WIN), :]
        r_out[row_of(rim_row), :] = r_out[row_of(rim_row), :] + msg[pl.ds(2 * WIN, WIN), :]
        s_out[row_of(edge_row), :] = s_out[row_of(edge_row), :] + msg[pl.ds(3 * WIN, WIN), :]
        s_out[row_of(rim_row), :] = s_out[row_of(rim_row), :] + msg[pl.ds(4 * WIN, WIN), :]
    for p in range(2):
        _, _, scale = damping(s_out[window(p, FIELDS), :], r_out[window(p, FIELDS), :])
        for field in range(GROUP):
            delta[window(p, field), :] = scale * r_out[window(p, field), :]
    delta[row_of(0), :] = lo[pl.ds(0, WIN), :]
    delta[row_of(7), :] = hi[pl.ds(0, WIN), :]
    half = GROUP * ROWS
    low_plane[...] = delta[pl.ds(0, half), :]
    high_plane[...] = delta[pl.ds(half, half), :]


def second_kernel(mixing, r_win, s_win, delta, partial):
    lane = iota((ROWS, CZ), 1)
    mix = [[mixing[v, w] for w in range(VARS)] for v in range(VARS)]
    for p in range(2):
        inverse, coef_c, scale = damping(s_win[window(p, FIELDS), :], r_win[window(p, FIELDS), :])
        for i in range(HERE):
            values = [delta[window(p, i * VARS + v), :] for v in range(VARS)]
            for v in range(VARS):
                field = i * VARS + v
                here = values[v]
                beside = jnp.where(lane == CZ - 1, 0.0, shift_lanes(here, -1))
                beside = beside + jnp.where(lane == 0, 0.0, shift_lanes(here, 1))
                beside = beside + shift_rows(here, -1) + shift_rows(here, 1)
                beside = beside + delta[window(1 - p, field), :]
                total = coef_c * (6.0 * here - beside)
                start = s_win[window(p, field), :] * inverse
                total = total + (jnp.tanh(start + here) - jnp.tanh(start))
                for w in range(VARS):
                    total = total + mix[v][w] * values[w]
                for j in range(HERE):
                    if j != i:
                        total = total + OWN[i][j] * delta[window(p, j * VARS + v), :]
                partial[window(p, field), :] = here + scale * (r_win[window(p, field), :] - total)
        partial[window(p, FIELDS), :] = coef_c


def final_kernel(partial, x_lo, x_hi, other, state, agg, corrected, change, fine, own, beside):
    for p in range(2):
        coef_c = partial[window(p, FIELDS), :]
        scale = 0.6 / (6.0 * coef_c + 2.0)
        halo = x_lo if p == 0 else x_hi
        for i in range(HERE):
            for v in range(VARS):
                field = i * VARS + v
                total = coef_c * halo[pl.ds(field * ROWS, ROWS), :]
                for j in range(HERE):
                    total = total - OTHER[i][j] * other[window(p, j * VARS + v), :]
                change[window(p, field), :] = partial[window(p, field), :] + scale * total
        change[window(p, FIELDS), :] = jnp.zeros((ROWS, CZ), F32)
    twice = (iota((CZ, NZ), 1) >> 1 == iota((CZ, NZ), 0)).astype(BF16)
    for half in range(2):
        fine[half] = pair_sums(change[...], twice[:, half * 128 : (half + 1) * 128])
    for half in range(2):
        rows = [fine[half, row_of(b + 1), :] for b in range(6)]
        for b in range(4):
            own[half, row_of(2 * b), :] = rows[b + 1]
            own[half, row_of(2 * b + 1), :] = rows[b + 1]
            beside[half, row_of(2 * b), :] = rows[b]
            beside[half, row_of(2 * b + 1), :] = rows[b + 2]
    for p in range(2):
        mask = moved_mask(agg, p)
        for half in range(2):
            lanes = pl.ds(half * 128, 128)
            moved = mask[:, half * 128 : (half + 1) * 128] > 0.0
            for field in range(FIELDS):
                kept = own[half, window(p, field), :]
                went = beside[half, window(p, field), :]
                corrected[tile(field, 2 * p), lanes] = state[tile(field, 2 * p), lanes] + kept
                corrected[tile(field, 2 * p + 1), lanes] = state[
                    tile(field, 2 * p + 1), lanes
                ] + jnp.where(moved, went, kept)


VMEM = pl.BlockSpec(memory_space=pltpu.VMEM)
SMEM = pl.BlockSpec(memory_space=pltpu.SMEM)


def call(kernel, outs, scratch, *args, scalars=0):
    return pl.pallas_call(
        kernel,
        out_shape=[jax.ShapeDtypeStruct(s, F32) for s in outs],
        in_specs=[SMEM] * scalars + [VMEM] * (len(args) - scalars),
        out_specs=[VMEM] * len(outs),
        scratch_shapes=[pltpu.VMEM(s, F32) for s in scratch],
        compiler_params=pltpu.CompilerParams(vmem_limit_bytes=40 * 1024 * 1024),
        name=kernel.__name__,
    )(*args)


def shards(state, forcing, coef, mixing, agglomerate):
    shape = state.shape
    fine = (FIELDS * PLANES * ROWS, NZ)
    wins = (WIN * ROWS, CZ)
    state = state.reshape(fine)
    forcing = forcing.reshape(fine)
    coef = coef.reshape(PLANES * ROWS, NZ)
    agg = agglomerate.reshape(PLANES * ROWS, NZ)

    def pairs(axis):
        up = [(i, i + 1) for i in range(lax.axis_size(axis) - 1)]
        return up, [(j, i) for i, j in up]

    sx_up, sx_down = pairs("sx")
    sy_up, sy_down = pairs("sy")
    swap = [(0, 1), (1, 0)]

    other = lax.ppermute(state, "hb", swap)
    halves = (2, FIELDS * PLANES * ROWS, 128)
    x_face = (FIELDS * ROWS, NZ)
    y_face = (FIELDS * PLANES, NZ)
    x_up, x_down, y_up, y_down = call(edges_kernel, [x_face, x_face, y_face, y_face], [halves], state)
    x_lo = lax.ppermute(x_up, "sx", sx_up)
    x_hi = lax.ppermute(x_down, "sx", sx_down)
    y_lo = lax.ppermute(y_up, "sy", sy_up)
    y_hi = lax.ppermute(y_down, "sy", sy_down)
    rows = (WIN * ROWS, NZ)
    rims = (2, WIN * ROWS, 128)
    partial, s_win = call(
        inner_kernel, [fine, wins], [rows, rims, wins], mixing, state, forcing, coef, agg, scalars=1
    )
    msg = (5 * WIN, CZ)
    residual, r_win, up, down = call(
        outer_kernel,
        [fine, wins, msg, msg],
        [rows, rims, wins, (8, 128), wins, halves, (2, PLANES * ROWS, 128)],
        partial, x_lo, x_hi, y_lo, y_hi, other, coef, agg, s_win,
    )
    lo = lax.ppermute(up, "sy", sy_up)
    hi = lax.ppermute(down, "sy", sy_down)
    plane = (GROUP * ROWS, CZ)
    r_win, s_win, delta, low, high = call(
        first_kernel, [wins, wins, wins, plane, plane], [], r_win, s_win, lo, hi
    )
    other_delta = lax.ppermute(delta, "hb", swap)
    d_lo = lax.ppermute(high, "sx", sx_up)
    d_hi = lax.ppermute(low, "sx", sx_down)
    (step,) = call(second_kernel, [wins], [], mixing, r_win, s_win, delta, scalars=1)
    (corrected,) = call(
        final_kernel,
        [fine],
        [wins, (2,) + wins, (2,) + wins, (2,) + wins],
        step, d_lo, d_hi, other_delta, state, agg,
    )
    return corrected.reshape(shape), residual.reshape(shape)


def solution(mesh):
    whole = P("hb", None, "sx", "sy", None)
    return jax.shard_map(
        shards,
        mesh=mesh,
        in_specs=(whole, whole, P("sx", "sy", None), P(), P("sx", "sy", None)),
        out_specs=(whole, whole),
        check_vma=False,
    )
```

time: 253 us -> 67.2 us (0.27)
  the two profiles are of different devices: /device:TPU:646 before, /device:TPU:62 now
where the time goes in v1:
time: 67.2 us; the launch traced here: 66.7 us
  starting transfers between devices  40 us (60%)
  waiting for transfers between devices  17.8 us (26%)
  Pallas kernels  4.49 us (7%)
  local copies, waits for them, and re-layouts  3.58 us (5%)
  between operations  0.81 us (1%)
    ppermute x1, starting transfers between devices, shards(): d_lo = lax.ppermute(high, 'sx', sx_up)  11.9 us
    ppermute x1, starting transfers between devices, shards(): y_lo = lax.ppermute(y_up, 'sy', sy_up)  8.31 us
    ppermute x1, waiting for transfers between devices, shards(): hi = lax.ppermute(down, 'sy', sy_down)  7.54 us
    ppermute x1, waiting for transfers between devices, shards(): d_hi = lax.ppermute(low, 'sx', sx_down)  5.53 us
    pallas_call x6, Pallas kernels, call(): pl.pallas_call(kernel, out_shape=[jax.ShapeDtypeStruct(s, F32) for s in o...  4.49 us
    ppermute x1, starting transfers between devices, shards(): x_lo = lax.ppermute(x_up, 'sx', sx_up)  4.33 us
    ppermute x1, waiting for transfers between devices, shards(): y_hi = lax.ppermute(y_down, 'sy', sy_down)  4.23 us
    ppermute x1, starting transfers between devices, shards(): lo = lax.ppermute(up, 'sy', sy_up)  3.61 us
  transfers between devices with their start and end apart: 10, of which 4 were waited for; matrix products, arithmetic and copies ran while one was open for 0% of the time, Pallas kernels for 3%

profile of v1, /device:TPU:62, one launch (start us, length us, event | category | flops | bytes accessed | tf_op | source)
XLA Modules:
  0.0 66.7 jit_solution(1888836417484649545)
XLA Ops:
  0.6 1.9 %collective-permute-start.4 = (f32[480,256]{1,0:T(8,128)}, f32[480,256]{1,0:T(8,128)S(1)}, u32[]{:S(2)}, u32[]{:S(2)}) collective-permute-start(f32[480,256]{1,0:T(8,128)} %bitcast.6), channel_id=1, source_target_pairs={{0,1},{1,0},{2,3},{3,2},{4,5},{5,4},{6,7},{7,6},{8,9},{9,8},{10,11... | collective-permute-start | bytes 1474568 | tf_op jit(solution)/shard_map/ppermute | solution.py:338
  2.6 1.0 %copy-done = f32[3,5,4,8,256]{4,3,2,1,0:T(8,128)S(1)} copy-done((f32[3,5,4,8,256]{4,3,2,1,0:T(8,128)S(1)}, f32[3,5,4,8,256]{4,3,2,1,0:T(8,128)}, u32[]{:S(2)}) %copy-start) | copy-done | bytes 491544
  3.6 0.1 edges_kernel.1
  3.7 4.3 %collective-permute-start = (f32[120,256]{1,0:T(8,128)S(1)}, f32[120,256]{1,0:T(8,128)S(1)}, u32[]{:S(2)}, u32[]{:S(2)}) collective-permute-start(f32[120,256]{1,0:T(8,128)S(1)} %get-tuple-element.18), channel_id=1, source_target_pairs={{0,64},{64,128},{128,192},{192,256},{256,320},{320,384},{384,448},... | collective-permute-start | bytes 368648 | tf_op jit(solution)/shard_map/ppermute | solution.py:343
  8.0 1.9 %collective-permute-start.1 = (f32[120,256]{1,0:T(8,128)S(1)}, f32[120,256]{1,0:T(8,128)S(1)}, u32[]{:S(2)}, u32[]{:S(2)}) collective-permute-start(f32[120,256]{1,0:T(8,128)S(1)} %get-tuple-element.19), channel_id=1, source_target_pairs={{64,0},{128,64},{192,128},{256,192},{320,256},{384,320},{448,384},... | collective-permute-start | bytes 368648 | tf_op jit(solution)/shard_map/ppermute | solution.py:344
  9.9 0.0 copy-start.7
  9.9 8.3 %collective-permute-start.2 = (f32[60,256]{1,0:T(8,128)S(1)}, f32[60,256]{1,0:T(8,128)S(1)}, u32[]{:S(2)}, u32[]{:S(2)}) collective-permute-start(f32[60,256]{1,0:T(8,128)S(1)} %get-tuple-element.20), channel_id=1, source_target_pairs={{0,2},{2,4},{4,6},{6,8},{8,10},{10,12},{12,14},{14,16},{16,18},{18... | collective-permute-start | bytes 184328 | tf_op jit(solution)/shard_map/ppermute | solution.py:345
  18.3 1.9 %collective-permute-start.3 = (f32[60,256]{1,0:T(8,128)S(1)}, f32[60,256]{1,0:T(8,128)S(1)}, u32[]{:S(2)}, u32[]{:S(2)}) collective-permute-start(f32[60,256]{1,0:T(8,128)S(1)} %get-tuple-element.21), channel_id=1, source_target_pairs={{2,0},{4,2},{6,4},{8,6},{10,8},{12,10},{14,12},{16,14},{18,16},{20... | collective-permute-start | bytes 184328 | tf_op jit(solution)/shard_map/ppermute | solution.py:346
  20.2 0.0 copy-start.2
  20.2 1.0 %copy-done.2 = f32[3,5,4,8,256]{4,3,2,1,0:T(8,128)S(1)} copy-done((f32[3,5,4,8,256]{4,3,2,1,0:T(8,128)S(1)}, f32[3,5,4,8,256]{4,3,2,1,0:T(8,128)}, u32[]{:S(2)}) %copy-start.2) | copy-done | bytes 491544
  21.3 0.8 %copy-done.3 = s32[4,8,256]{2,1,0:T(8,128)S(1)} copy-done((s32[4,8,256]{2,1,0:T(8,128)S(1)}, s32[4,8,256]{2,1,0:T(8,128)}, u32[]{:S(2)}) %copy-start.3) | copy-done | bytes 32792
  22.0 0.8 %copy-done.5 = f32[4,8,256]{2,1,0:T(8,128)S(1)} copy-done((f32[4,8,256]{2,1,0:T(8,128)S(1)}, f32[4,8,256]{2,1,0:T(8,128)}, u32[]{:S(2)}) %copy-start.5) | copy-done | bytes 32792
  22.8 1.3 %inner_kernel.1 = (f32[480,256]{1,0:T(8,128)S(1)}, f32[256,128]{1,0:T(8,128)S(1)}) custom-call(f32[5,5]{1,0:T(8,128)S(1)} %copy-done.7, f32[480,256]{1,0:T(8,128)S(1)} %bitcast.8, f32[480,256]{1,0:T(8,128)S(1)} %bitcast.10, f32[32,256]{1,0:T(8,128)S(1)} %bitcast.14, s32[32,256]{1,0:T(8,128)S(1)} %bitcast.11), custom_call_target="tpu_custom_call" | custom-call | tf_op jit(solution)/shard_map/inner_kernel/pallas_call | solution.py:310
  24.1 0.0 collective-permute-done.2.y_lo
  24.1 4.2 %collective-permute-done.3.y_hi = f32[60,256]{1,0:T(8,128)S(1)} collective-permute-done((f32[60,256]{1,0:T(8,128)S(1)}, f32[60,256]{1,0:T(8,128)S(1)}, u32[]{:S(2)}, u32[]{:S(2)}) %collective-permute-start.3) | collective-permute-done | bytes 61472 | tf_op jit(solution)/shard_map/ppermute | solution.py:346
  28.3 0.0 collective-permute-done.x_lo
  28.3 0.0 collective-permute-done.1.x_hi
  28.3 0.0 collective-permute-done.4.other
  28.4 1.1 %outer_kernel.1 = (f32[480,256]{1,0:T(8,128)}, f32[256,128]{1,0:T(8,128)S(1)}, f32[160,128]{1,0:T(8,128)S(1)}, f32[160,128]{1,0:T(8,128)S(1)}) custom-call(f32[480,256]{1,0:T(8,128)S(1)} %get-tuple-element.17.partial, f32[120,256]{1,0:T(8,128)S(1)} %collective-permute-done.x_lo, f32[120,256]{1,0:T(8,128)S(1)} %collective-permute-done.1.x_hi, ...), custom_call_target="tpu_custom_call" | custom-call | tf_op jit(solution)/shard_map/outer_kernel/pallas_call | solution.py:310
  29.4 3.6 %collective-permute-start.5 = (f32[160,128]{1,0:T(8,128)S(1)}, f32[160,128]{1,0:T(8,128)S(1)}, u32[]{:S(2)}, u32[]{:S(2)}) collective-permute-start(f32[160,128]{1,0:T(8,128)S(1)} %get-tuple-element.24), channel_id=1, source_target_pairs={{0,2},{2,4},{4,6},{6,8},{8,10},{10,12},{12,14},{14,16},{16,18},{18... | collective-permute-start | bytes 245768 | tf_op jit(solution)/shard_map/ppermute | solution.py:359
  33.1 2.2 %collective-permute-start.6 = (f32[160,128]{1,0:T(8,128)S(1)}, f32[160,128]{1,0:T(8,128)S(1)}, u32[]{:S(2)}, u32[]{:S(2)}) collective-permute-start(f32[160,128]{1,0:T(8,128)S(1)} %get-tuple-element.25), channel_id=1, source_target_pairs={{2,0},{4,2},{6,4},{8,6},{10,8},{12,10},{14,12},{16,14},{18,16},{20... | collective-permute-start | bytes 245768 | tf_op jit(solution)/shard_map/ppermute | solution.py:360
  35.3 0.5 collective-permute-done.5.lo
  35.8 7.5 %collective-permute-done.6.hi = f32[160,128]{1,0:T(8,128)S(1)} collective-permute-done((f32[160,128]{1,0:T(8,128)S(1)}, f32[160,128]{1,0:T(8,128)S(1)}, u32[]{:S(2)}, u32[]{:S(2)}) %collective-permute-start.6) | collective-permute-done | bytes 81952 | tf_op jit(solution)/shard_map/ppermute | solution.py:360
  43.3 0.1 first_kernel.1
  43.4 1.9 %collective-permute-start.9 = (f32[256,128]{1,0:T(8,128)S(1)}, f32[256,128]{1,0:T(8,128)S(1)}, u32[]{:S(2)}, u32[]{:S(2)}) collective-permute-start(f32[256,128]{1,0:T(8,128)S(1)} %get-tuple-element.28.delta), channel_id=1, source_target_pairs={{0,1},{1,0},{2,3},{3,2},{4,5},{5,4},{6,7},{7,6},{8,9},{9,8},{10,11... | collective-permute-start | bytes 393224 | tf_op jit(solution)/shard_map/ppermute | solution.py:365
  45.3 11.9 %collective-permute-start.7 = (f32[128,128]{1,0:T(8,128)S(1)}, f32[128,128]{1,0:T(8,128)S(1)}, u32[]{:S(2)}, u32[]{:S(2)}) collective-permute-start(f32[128,128]{1,0:T(8,128)S(1)} %get-tuple-element.29), channel_id=1, source_target_pairs={{0,64},{64,128},{128,192},{192,256},{256,320},{320,384},{384,448},... | collective-permute-start | bytes 196616 | tf_op jit(solution)/shard_map/ppermute | solution.py:366
  57.2 1.9 %collective-permute-start.8 = (f32[128,128]{1,0:T(8,128)S(1)}, f32[128,128]{1,0:T(8,128)S(1)}, u32[]{:S(2)}, u32[]{:S(2)}) collective-permute-start(f32[128,128]{1,0:T(8,128)S(1)} %get-tuple-element.30), channel_id=1, source_target_pairs={{64,0},{128,64},{192,128},{256,192},{320,256},{384,320},{448,384},... | collective-permute-start | bytes 196616 | tf_op jit(solution)/shard_map/ppermute | solution.py:367
  59.2 0.8 %second_kernel.1.partial = f32[256,128]{1,0:T(8,128)S(1)} custom-call(f32[5,5]{1,0:T(8,128)S(1)} %copy-done.7, f32[256,128]{1,0:T(8,128)S(1)} %get-tuple-element.26.r_win, f32[256,128]{1,0:T(8,128)S(1)} %get-tuple-element.27.s_win, f32[256,128]{1,0:T(8,128)S(1)} %get-tuple-element.28.delta), custom_call_target="tpu_custom_call" | custom-call | tf_op jit(solution)/shard_map/second_kernel/pallas_call | solution.py:310
  60.0 0.0 collective-permute-done.7.x_lo
  60.0 5.5 %collective-permute-done.8.x_hi = f32[128,128]{1,0:T(8,128)S(1)} collective-permute-done((f32[128,128]{1,0:T(8,128)S(1)}, f32[128,128]{1,0:T(8,128)S(1)}, u32[]{:S(2)}, u32[]{:S(2)}) %collective-permute-start.8) | collective-permute-done | bytes 65568 | tf_op jit(solution)/shard_map/ppermute | solution.py:367
  65.5 0.0 collective-permute-done.9.other
  65.5 1.1 %final_kernel.1 = f32[480,256]{1,0:T(8,128)} custom-call(f32[256,128]{1,0:T(8,128)S(1)} %second_kernel.1.partial, f32[128,128]{1,0:T(8,128)S(1)} %collective-permute-done.7.x_lo, f32[128,128]{1,0:T(8,128)S(1)} %collective-permute-done.8.x_hi, f32[256,128]{1,0:T(8,128)S(1)} %collective-permute-done.9.other, f32[480,256]{1,0:T(8,128)S(1)} %bitcast.9, ...), custom_call_target="tpu_custom_call" | custom-call | tf_op jit(solution)/shard_map/final_kernel/pallas_call | solution.py:310
  (10 shorter events, 0.0 us)
Async XLA Ops:
  0.6 27.7 %collective-permute-start.4 = (f32[480,256]{1,0:T(8,128)}, f32[480,256]{1,0:T(8,128)S(1)}, u32[]{:S(2)}, u32[]{:S(2)}) collective-permute-start(f32[480,256]{1,0:T(8,128)} %bitcast.6), channel_id=1, source_target_pairs={{0,1},{1,0},{2,3},{3,2},{4,5},{5,4},{6,7},{7,6},{8,9},{9,8},{10,11... | collective-permute-start | bytes 1474568 | tf_op jit(solution)/shard_map/ppermute | solution.py:338
  2.6 1.0 %copy-start = (f32[3,5,4,8,256]{4,3,2,1,0:T(8,128)S(1)}, f32[3,5,4,8,256]{4,3,2,1,0:T(8,128)}, u32[]{:S(2)}) copy-start(f32[3,5,4,8,256]{4,3,2,1,0:T(8,128)} %param.5) | copy-start | bytes 1474564
  3.6 16.6 %copy-start.1 = (f32[3,5,4,8,256]{4,3,2,1,0:T(8,128)S(1)}, f32[3,5,4,8,256]{4,3,2,1,0:T(8,128)}, u32[]{:S(2)}) copy-start(f32[3,5,4,8,256]{4,3,2,1,0:T(8,128)} %param.5) | copy-start | bytes 1474564
  3.7 24.7 %collective-permute-start = (f32[120,256]{1,0:T(8,128)S(1)}, f32[120,256]{1,0:T(8,128)S(1)}, u32[]{:S(2)}, u32[]{:S(2)}) collective-permute-start(f32[120,256]{1,0:T(8,128)S(1)} %get-tuple-element.18), channel_id=1, source_target_pairs={{0,64},{64,128},{128,192},{192,256},{256,320},{320,384},{384,448},... | collective-permute-start | bytes 368648 | tf_op jit(solution)/shard_map/ppermute | solution.py:343
  8.0 20.3 %collective-permute-start.1 = (f32[120,256]{1,0:T(8,128)S(1)}, f32[120,256]{1,0:T(8,128)S(1)}, u32[]{:S(2)}, u32[]{:S(2)}) collective-permute-start(f32[120,256]{1,0:T(8,128)S(1)} %get-tuple-element.19), channel_id=1, source_target_pairs={{64,0},{128,64},{192,128},{256,192},{320,256},{384,320},{448,384},... | collective-permute-start | bytes 368648 | tf_op jit(solution)/shard_map/ppermute | solution.py:344
  9.9 10.3 %copy-start.7 = (f32[5,5]{1,0:T(8,128)S(1)}, f32[5,5]{1,0:T(8,128)}, u32[]{:S(2)}) copy-start(f32[5,5]{1,0:T(8,128)} %mixing.3) | copy-start | bytes 304
  9.9 14.1 %collective-permute-start.2 = (f32[60,256]{1,0:T(8,128)S(1)}, f32[60,256]{1,0:T(8,128)S(1)}, u32[]{:S(2)}, u32[]{:S(2)}) collective-permute-start(f32[60,256]{1,0:T(8,128)S(1)} %get-tuple-element.20), channel_id=1, source_target_pairs={{0,2},{2,4},{4,6},{6,8},{8,10},{10,12},{12,14},{14,16},{16,18},{18... | collective-permute-start | bytes 184328 | tf_op jit(solution)/shard_map/ppermute | solution.py:345
  18.3 10.1 %collective-permute-start.3 = (f32[60,256]{1,0:T(8,128)S(1)}, f32[60,256]{1,0:T(8,128)S(1)}, u32[]{:S(2)}, u32[]{:S(2)}) collective-permute-start(f32[60,256]{1,0:T(8,128)S(1)} %get-tuple-element.21), channel_id=1, source_target_pairs={{2,0},{4,2},{6,4},{8,6},{10,8},{12,10},{14,12},{16,14},{18,16},{20... | collective-permute-start | bytes 184328 | tf_op jit(solution)/shard_map/ppermute | solution.py:346
  20.2 1.0 %copy-start.2 = (f32[3,5,4,8,256]{4,3,2,1,0:T(8,128)S(1)}, f32[3,5,4,8,256]{4,3,2,1,0:T(8,128)}, u32[]{:S(2)}) copy-start(f32[3,5,4,8,256]{4,3,2,1,0:T(8,128)} %param.6) | copy-start | bytes 1474564
  21.3 0.8 %copy-start.3 = (s32[4,8,256]{2,1,0:T(8,128)S(1)}, s32[4,8,256]{2,1,0:T(8,128)}, u32[]{:S(2)}) copy-start(s32[4,8,256]{2,1,0:T(8,128)} %param.9) | copy-start | bytes 98308
  22.0 0.8 %copy-start.5 = (f32[4,8,256]{2,1,0:T(8,128)S(1)}, f32[4,8,256]{2,1,0:T(8,128)}, u32[]{:S(2)}) copy-start(f32[4,8,256]{2,1,0:T(8,128)} %param.7) | copy-start | bytes 98308
  22.8 5.6 %copy-start.4 = (s32[4,8,256]{2,1,0:T(8,128)S(1)}, s32[4,8,256]{2,1,0:T(8,128)}, u32[]{:S(2)}) copy-start(s32[4,8,256]{2,1,0:T(8,128)} %param.9) | copy-start | bytes 98308
  22.8 5.6 %copy-start.6 = (f32[4,8,256]{2,1,0:T(8,128)S(1)}, f32[4,8,256]{2,1,0:T(8,128)}, u32[]{:S(2)}) copy-start(f32[4,8,256]{2,1,0:T(8,128)} %param.7) | copy-start | bytes 98308
  29.4 6.3 %collective-permute-start.5 = (f32[160,128]{1,0:T(8,128)S(1)}, f32[160,128]{1,0:T(8,128)S(1)}, u32[]{:S(2)}, u32[]{:S(2)}) collective-permute-start(f32[160,128]{1,0:T(8,128)S(1)} %get-tuple-element.24), channel_id=1, source_target_pairs={{0,2},{2,4},{4,6},{6,8},{8,10},{10,12},{12,14},{14,16},{16,18},{18... | collective-permute-start | bytes 245768 | tf_op jit(solution)/shard_map/ppermute | solution.py:359
  33.1 10.2 %collective-permute-start.6 = (f32[160,128]{1,0:T(8,128)S(1)}, f32[160,128]{1,0:T(8,128)S(1)}, u32[]{:S(2)}, u32[]{:S(2)}) collective-permute-start(f32[160,128]{1,0:T(8,128)S(1)} %get-tuple-element.25), channel_id=1, source_target_pairs={{2,0},{4,2},{6,4},{8,6},{10,8},{12,10},{14,12},{16,14},{18,16},{20... | collective-permute-start | bytes 245768 | tf_op jit(solution)/shard_map/ppermute | solution.py:360
  43.4 22.1 %collective-permute-start.9 = (f32[256,128]{1,0:T(8,128)S(1)}, f32[256,128]{1,0:T(8,128)S(1)}, u32[]{:S(2)}, u32[]{:S(2)}) collective-permute-start(f32[256,128]{1,0:T(8,128)S(1)} %get-tuple-element.28.delta), channel_id=1, source_target_pairs={{0,1},{1,0},{2,3},{3,2},{4,5},{5,4},{6,7},{7,6},{8,9},{9,8},{10,11... | collective-permute-start | bytes 393224 | tf_op jit(solution)/shard_map/ppermute | solution.py:365
  45.3 14.6 %collective-permute-start.7 = (f32[128,128]{1,0:T(8,128)S(1)}, f32[128,128]{1,0:T(8,128)S(1)}, u32[]{:S(2)}, u32[]{:S(2)}) collective-permute-start(f32[128,128]{1,0:T(8,128)S(1)} %get-tuple-element.29), channel_id=1, source_target_pairs={{0,64},{64,128},{128,192},{192,256},{256,320},{320,384},{384,448},... | collective-permute-start | bytes 196616 | tf_op jit(solution)/shard_map/ppermute | solution.py:366
  57.2 8.3 %collective-permute-start.8 = (f32[128,128]{1,0:T(8,128)S(1)}, f32[128,128]{1,0:T(8,128)S(1)}, u32[]{:S(2)}, u32[]{:S(2)}) collective-permute-start(f32[128,128]{1,0:T(8,128)S(1)} %get-tuple-element.30), channel_id=1, source_target_pairs={{64,0},{128,64},{192,128},{256,192},{320,256},{384,320},{448,384},... | collective-permute-start | bytes 196616 | tf_op jit(solution)/shard_map/ppermute | solution.py:367

commit v2 on v1

v2 whole, which is shorter than its diff:
```python
import functools

import jax
import jax.numpy as jnp
import numpy as np
from jax import lax
from jax.experimental import pallas as pl
from jax.experimental.pallas import tpu as pltpu
from jax.sharding import PartitionSpec as P

INST = 6
HERE = 3
VARS = 5
FIELDS = HERE * VARS
PLANES = 4
ROWS = 8
NZ = 256
CZ = 128
GROUP = 16
WIN = 2 * GROUP
F32 = jnp.float32
BF16 = jnp.bfloat16


def spectral_matrix():
    rows = np.arange(INST)[:, None]
    cols = np.arange(INST)[None, :]
    diff = rows - cols
    same = diff == 0
    angle = np.where(same, 1.0, np.pi * diff / INST).astype(np.float32)
    signs = np.where(diff % 2 == 0, 1.0, -1.0).astype(np.float32)
    return np.where(same, 0.0, 0.5 * signs * np.cos(angle) / np.sin(angle))


SPECTRAL = spectral_matrix()
OWN = [[float(SPECTRAL[i, j]) for j in range(HERE)] for i in range(HERE)]
OTHER = [[float(SPECTRAL[i, j + HERE]) for j in range(HERE)] for i in range(HERE)]


def tile(field, plane):
    return pl.ds((field * PLANES + plane) * ROWS, ROWS)


def window(plane, field):
    return pl.ds((plane * GROUP + field) * ROWS, ROWS)


def row_of(index):
    return pl.ds(index, WIN, stride=ROWS)


def iota(shape, dim):
    return lax.broadcasted_iota(jnp.int32, shape, dim)


def moved_mask(agg_ref, plane):
    block = agg_ref[pl.ds((2 * plane + 1) * ROWS, ROWS), :]
    own = iota((ROWS, NZ), 0) >> 1
    return (((block >> 7) ^ own) & 1).astype(F32)


def pair_sums(values, ones):
    high = values.astype(BF16)
    low = (values - high.astype(F32)).astype(BF16)
    return jnp.dot(high, ones, preferred_element_type=F32) + jnp.dot(
        low, ones, preferred_element_type=F32
    )


def shift_rows(value, amount):
    return pltpu.roll(value, amount % value.shape[0], 0)


def shift_lanes(value, amount):
    return pltpu.roll(value, amount % value.shape[1], 1)


def even_index(axis):
    return lax.axis_index(axis) % 2 == 0


def choose(flag, value, other):
    return jnp.where(jnp.full(value.shape, flag.astype(jnp.int32)) > 0, value, other)


def edges_kernel(
    state_in, forcing_in, coef_in, agg_in,
    yb, xb, xa, ya, state, forcing, coef, agg, s_win,
    halves, sums, rims, summed, sems,
):
    pairs = ((state_in, state), (coef_in, coef), (agg_in, agg), (forcing_in, forcing))
    copies = [pltpu.make_async_copy(s, d, sems.at[n]) for n, (s, d) in enumerate(pairs)]
    for copy in copies:
        copy.start()
    for copy in copies[:3]:
        copy.wait()
    even_x, even_y = (even_index("sx"), even_index("sy"))
    for field in range(FIELDS):
        high, low = (state[tile(field, PLANES - 1), :], state[tile(field, 0), :])
        xa[pl.ds(field * ROWS, ROWS), :] = choose(even_x, high, low)
        xb[pl.ds(field * ROWS, ROWS), :] = choose(even_x, low, high)
    count = FIELDS * PLANES
    for half in range(2):
        lanes = pl.ds(half * 128, 128)
        halves[half] = state[:, lanes]
        high = halves[half, pl.ds(ROWS - 1, count, stride=ROWS), :]
        low = halves[half, pl.ds(0, count, stride=ROWS), :]
        ya[pl.ds(0, count), lanes] = choose(even_y, high, low)
        yb[pl.ds(0, count), lanes] = choose(even_y, low, high)
        nothing = jnp.zeros((64 - count, 128), F32)
        ya[pl.ds(count, 64 - count), lanes] = nothing
        yb[pl.ds(count, 64 - count), lanes] = nothing
    restrict(state, lambda x: coef[pl.ds(x * ROWS, ROWS), :], agg, s_win, sums, rims, summed)
    for half, (above, below) in enumerate(((5, 2), (6, 1))):
        lanes = pl.ds(half * 128, 128)
        high, low = (s_win[row_of(above), :], s_win[row_of(below), :])
        ya[pl.ds(64, WIN), lanes] = choose(even_y, high, low)
        yb[pl.ds(64, WIN), lanes] = choose(even_y, low, high)
    copies[3].wait()


def split_moved(even, odd, mask, parity, inside):
    moved = odd * mask
    beside = jnp.where(parity, shift_rows(moved, -1), shift_rows(moved, 1))
    return even + (odd - moved) + jnp.where(inside, beside, 0.0), beside


def fill_windows(out, sums, rims, summed, ones):
    summed[pl.ds(0, WIN * ROWS), :] = pair_sums(sums[...], ones)
    first = jnp.concatenate([rims[h, row_of(0), :] for h in range(2)], axis=1)
    last = jnp.concatenate([rims[h, row_of(ROWS - 1), :] for h in range(2)], axis=1)
    rim = pair_sums(jnp.concatenate([first, last], axis=0), ones)
    nothing = jnp.zeros((WIN, CZ), F32)
    out[row_of(0), :] = nothing
    out[row_of(7), :] = nothing
    out[row_of(1), :] = rim[WIN:]
    out[row_of(6), :] = rim[:WIN]
    for b in range(4):
        out[row_of(b + 2), :] = summed[row_of(2 * b), :] + summed[row_of(2 * b + 1), :]


def restrict(fine, last, agg, out, sums, rims, summed):
    row = iota((ROWS, NZ), 0)
    parity = row % 2 == 1
    inside = (row > 0) & (row < ROWS - 1)
    for p in range(2):
        mask = moved_mask(agg, p)
        for field in range(GROUP):
            if field < FIELDS:
                even, odd = (fine[tile(field, 2 * p), :], fine[tile(field, 2 * p + 1), :])
            else:
                even, odd = (last(2 * p), last(2 * p + 1))
            kept, beside = split_moved(even, odd, mask, parity, inside)
            sums[window(p, field), :] = kept
            for half in range(2):
                rims[half, window(p, field), :] = beside[:, half * 128 : (half + 1) * 128]
    fill_windows(out, sums, rims, summed, pair_matrix())


def pair_matrix():
    return (iota((NZ, CZ), 0) >> 1 == iota((NZ, CZ), 1)).astype(BF16)


def inner_kernel(mixing, state, forcing, coef, partial):
    lane = iota((ROWS, NZ), 1)
    row = iota((ROWS, NZ), 0)
    mix = [[mixing[v, w] for w in range(VARS)] for v in range(VARS)]
    for x in range(PLANES):
        c = coef[pl.ds(x * ROWS, ROWS), :]
        for i in range(HERE):
            values = [state[tile(i * VARS + v, x), :] for v in range(VARS)]
            for v in range(VARS):
                field = i * VARS + v
                here = values[v]
                beside = jnp.where(lane == NZ - 1, 0.0, shift_lanes(here, -1))
                beside = beside + jnp.where(lane == 0, 0.0, shift_lanes(here, 1))
                beside = beside + jnp.where(row == ROWS - 1, 0.0, shift_rows(here, -1))
                beside = beside + jnp.where(row == 0, 0.0, shift_rows(here, 1))
                if x > 0:
                    beside = beside + state[tile(field, x - 1), :]
                if x < PLANES - 1:
                    beside = beside + state[tile(field, x + 1), :]
                total = c * (6.0 * here - beside) + jnp.tanh(here)
                for w in range(VARS):
                    total = total + mix[v][w] * values[w]
                for j in range(HERE):
                    if j != i:
                        total = total + OWN[i][j] * state[tile(j * VARS + v, x), :]
                partial[tile(field, x), :] = forcing[tile(field, x), :] - total


def damping(coef_sum, count):
    inverse = jnp.where(count > 0.0, 1.0 / jnp.maximum(count, 1.0), 0.0)
    coef_c = coef_sum * inverse
    return inverse, coef_c, 0.6 / (6.0 * coef_c + 2.0)


def outer_kernel(
    partial, xa, xb, ya, yb, other, coef, agg, s_in,
    mb, ma, residual, r_win, s_win, sums, rims, summed, edge, scaled, halves, coefs,
):
    even_x, even_y = (even_index("sx"), even_index("sy"))
    for x in range(PLANES):
        c = coef[pl.ds(x * ROWS, ROWS), :]
        for i in range(HERE):
            for v in range(VARS):
                field = i * VARS + v
                face = pl.ds(field * ROWS, ROWS)
                total = partial[tile(field, x), :]
                for j in range(HERE):
                    total = total - OTHER[i][j] * other[tile(j * VARS + v, x), :]
                if x == 0:
                    total = total + c * choose(even_x, xb[face, :], xa[face, :])
                if x == PLANES - 1:
                    total = total + c * choose(even_x, xa[face, :], xb[face, :])
                for half in range(2):
                    halves[half, tile(field, x), :] = total[:, half * 128 : (half + 1) * 128]
    count = FIELDS * PLANES
    for half in range(2):
        lanes = pl.ds(half * 128, 128)
        coefs[half] = coef[:, lanes]
        at_a, at_b = (ya[pl.ds(0, count), lanes], yb[pl.ds(0, count), lanes])
        for y, halo in ((0, choose(even_y, at_b, at_a)), (ROWS - 1, choose(even_y, at_a, at_b))):
            c4 = coefs[half, pl.ds(y, PLANES, stride=ROWS), :]
            edge[pl.ds(0, PLANES), :] = c4
            edge[pl.ds(PLANES, PLANES), :] = c4
            c8 = edge[...]
            c60 = jnp.concatenate([c8] * (count // 8) + [c8[: count % 8]], axis=0)
            rows = pl.ds(y, count, stride=ROWS)
            halves[half, rows, :] = halves[half, rows, :] + c60 * halo
        residual[:, lanes] = halves[half]
    restrict(residual, lambda x: jnp.ones((ROWS, NZ), F32), agg, r_win, sums, rims, summed)
    s_win[...] = s_in[...]
    for half, (above, below) in enumerate(((6, 1), (5, 2))):
        lanes = pl.ds(half * 128, 128)
        at_a, at_b = (ya[pl.ds(64, WIN), lanes], yb[pl.ds(64, WIN), lanes])
        s_win[row_of(below), :] = s_win[row_of(below), :] + choose(even_y, at_b, at_a)
        s_win[row_of(above), :] = s_win[row_of(above), :] + choose(even_y, at_a, at_b)
    for p in range(2):
        _, _, scale = damping(s_win[window(p, FIELDS), :], r_win[window(p, FIELDS), :])
        for field in range(GROUP):
            scaled[window(p, field), :] = scale * r_win[window(p, field), :]
    pieces = ((scaled, 4, 3), (r_win, 5, 2), (r_win, 6, 1))
    for n, (ref, above, below) in enumerate(pieces):
        high, low = (ref[row_of(above), :], ref[row_of(below), :])
        ma[pl.ds(n * WIN, WIN), :] = choose(even_y, high, low)
        mb[pl.ds(n * WIN, WIN), :] = choose(even_y, low, high)


def store_kernel(values, r_in, out, r_out, sems):
    copy = pltpu.make_async_copy(values, out, sems.at[0])
    copy.start()
    r_out[...] = r_in[...]
    copy.wait()


EDGE_ROWS = 6


def first_kernel(r_in, s_win, ma, mb, xb, xa, delta, r_win):
    even_x, even_y = (even_index("sx"), even_index("sy"))
    r_win[...] = r_in[...]
    pieces = []
    for n in range(3):
        at_a, at_b = (ma[pl.ds(n * WIN, WIN), :], mb[pl.ds(n * WIN, WIN), :])
        pieces.append((choose(even_y, at_b, at_a), choose(even_y, at_a, at_b)))
    for n, below, above in ((1, 1, 6), (2, 2, 5)):
        r_win[row_of(below), :] = r_win[row_of(below), :] + pieces[n][0]
        r_win[row_of(above), :] = r_win[row_of(above), :] + pieces[n][1]
    for p in range(2):
        _, _, scale = damping(s_win[window(p, FIELDS), :], r_win[window(p, FIELDS), :])
        for field in range(GROUP):
            delta[window(p, field), :] = scale * r_win[window(p, field), :]
    delta[row_of(0), :] = pieces[0][0]
    delta[row_of(7), :] = pieces[0][1]
    for r in range(EDGE_ROWS):
        low = delta[pl.ds(r + 1, GROUP, stride=ROWS), :]
        high = delta[pl.ds(GROUP * ROWS + r + 1, GROUP, stride=ROWS), :]
        xa[pl.ds(r * GROUP, GROUP), :] = choose(even_x, high, low)
        xb[pl.ds(r * GROUP, GROUP), :] = choose(even_x, low, high)


def second_kernel(mixing, r_win, s_win, delta, partial):
    lane = iota((ROWS, CZ), 1)
    mix = [[mixing[v, w] for w in range(VARS)] for v in range(VARS)]
    for p in range(2):
        inverse, coef_c, scale = damping(s_win[window(p, FIELDS), :], r_win[window(p, FIELDS), :])
        for i in range(HERE):
            values = [delta[window(p, i * VARS + v), :] for v in range(VARS)]
            for v in range(VARS):
                field = i * VARS + v
                here = values[v]
                beside = jnp.where(lane == CZ - 1, 0.0, shift_lanes(here, -1))
                beside = beside + jnp.where(lane == 0, 0.0, shift_lanes(here, 1))
                beside = beside + shift_rows(here, -1) + shift_rows(here, 1)
                beside = beside + delta[window(1 - p, field), :]
                total = coef_c * (6.0 * here - beside)
                start = s_win[window(p, field), :] * inverse
                total = total + (jnp.tanh(start + here) - jnp.tanh(start))
                for w in range(VARS):
                    total = total + mix[v][w] * values[w]
                for j in range(HERE):
                    if j != i:
                        total = total + OWN[i][j] * delta[window(p, j * VARS + v), :]
                partial[window(p, field), :] = here + scale * (r_win[window(p, field), :] - total)
        partial[window(p, FIELDS), :] = coef_c


def final_kernel(
    partial, xa, xb, other, state, agg, corrected, change, fine, own, beside, halos, result, sems
):
    even_x = even_index("sx")
    for r in range(EDGE_ROWS):
        at_a, at_b = (xa[pl.ds(r * GROUP, GROUP), :], xb[pl.ds(r * GROUP, GROUP), :])
        rows = pl.ds(r + 1, GROUP, stride=ROWS)
        halos[0, rows, :] = choose(even_x, at_b, at_a)
        halos[1, rows, :] = choose(even_x, at_a, at_b)
    for p in range(2):
        for r in (0, ROWS - 1):
            halos[p, pl.ds(r, GROUP, stride=ROWS), :] = jnp.zeros((GROUP, CZ), F32)
    for p in range(2):
        coef_c = partial[window(p, FIELDS), :]
        scale = 0.6 / (6.0 * coef_c + 2.0)
        for i in range(HERE):
            for v in range(VARS):
                field = i * VARS + v
                total = coef_c * halos[p, pl.ds(field * ROWS, ROWS), :]
                for j in range(HERE):
                    total = total - OTHER[i][j] * other[window(p, j * VARS + v), :]
                change[window(p, field), :] = partial[window(p, field), :] + scale * total
        change[window(p, FIELDS), :] = jnp.zeros((ROWS, CZ), F32)
    twice = (iota((CZ, NZ), 1) >> 1 == iota((CZ, NZ), 0)).astype(BF16)
    for half in range(2):
        fine[half] = pair_sums(change[...], twice[:, half * 128 : (half + 1) * 128])
    for half in range(2):
        rows = [fine[half, row_of(b + 1), :] for b in range(6)]
        for b in range(4):
            own[half, row_of(2 * b), :] = rows[b + 1]
            own[half, row_of(2 * b + 1), :] = rows[b + 1]
            beside[half, row_of(2 * b), :] = rows[b]
            beside[half, row_of(2 * b + 1), :] = rows[b + 2]
    masks = [moved_mask(agg, p) > 0.0 for p in range(2)]
    copies = []
    for i in range(HERE):
        for field in range(i * VARS, (i + 1) * VARS):
            for p in range(2):
                for half in range(2):
                    lanes = pl.ds(half * 128, 128)
                    moved = masks[p][:, half * 128 : (half + 1) * 128]
                    kept = own[half, window(p, field), :]
                    went = beside[half, window(p, field), :]
                    even, odd = (tile(field, 2 * p), tile(field, 2 * p + 1))
                    result[even, lanes] = state[even, lanes] + kept
                    result[odd, lanes] = state[odd, lanes] + jnp.where(moved, went, kept)
        rows = pl.ds(i * VARS * PLANES * ROWS, VARS * PLANES * ROWS)
        copies.append(pltpu.make_async_copy(result.at[rows, :], corrected.at[rows, :], sems.at[i]))
        copies[-1].start()
    for copy in copies:
        copy.wait()


VMEM = pl.BlockSpec(memory_space=pltpu.VMEM)
SMEM = pl.BlockSpec(memory_space=pltpu.SMEM)
HBM = pl.BlockSpec(memory_space=pltpu.HBM)


def call(kernel, outs, scratch, *args, spaces=(), out_space=VMEM, sems=0):
    spaces = list(spaces) + [VMEM] * (len(args) - len(spaces))
    args = [
        pltpu.with_memory_space_constraint(a, pltpu.HBM) if s is HBM else a
        for a, s in zip(args, spaces)
    ]
    outs = [o if hasattr(o, "dtype") else jax.ShapeDtypeStruct(o, F32) for o in outs]
    return pl.pallas_call(
        kernel,
        out_shape=outs,
        in_specs=spaces,
        out_specs=out_space if isinstance(out_space, list) else [out_space] * len(outs),
        scratch_shapes=[pltpu.VMEM(s, F32) for s in scratch]
        + ([pltpu.SemaphoreType.DMA((sems,))] if sems else []),
        compiler_params=pltpu.CompilerParams(vmem_limit_bytes=40 * 1024 * 1024),
        name=kernel.__name__,
    )(*args)


def swap_pairs(axis, first):
    size = lax.axis_size(axis)
    up = [(i, i + 1) for i in range(first, size - 1, 2)]
    return up + [(j, i) for i, j in up]


def shards(state, forcing, coef, mixing, agglomerate):
    shape = state.shape
    fine = (FIELDS * PLANES * ROWS, NZ)
    wins = (WIN * ROWS, CZ)
    state = state.reshape(fine)
    forcing = forcing.reshape(fine)
    coef = coef.reshape(PLANES * ROWS, NZ)
    agg = agglomerate.reshape(PLANES * ROWS, NZ)

    def swap(value, axis, first=0):
        return lax.ppermute(value, axis, swap_pairs(axis, first))

    halves = (2, FIELDS * PLANES * ROWS, 128)
    sums = (WIN * ROWS, NZ)
    rims = (2, WIN * ROWS, 128)
    x_face = (FIELDS * ROWS, NZ)
    y_face = (64 + WIN, NZ)
    yb, xb, xa, ya, state, forcing, coef, agg, s_win = call(
        edges_kernel,
        [y_face, x_face, x_face, y_face, fine, fine, coef.shape, agg, wins],
        [halves, sums, rims, wins],
        state, forcing, coef, agg,
        spaces=[HBM] * 4,
        sems=4,
    )
    yb = swap(yb, "sy", 1)
    xb = swap(xb, "sx", 1)
    xa = swap(xa, "sx")
    ya = swap(ya, "sy")
    other = swap(state, "hb")
    (partial,) = call(inner_kernel, [fine], [], mixing, state, forcing, coef, spaces=[SMEM])
    msg = (3 * WIN, CZ)
    mb, ma, residual, r_win, s_win = call(
        outer_kernel,
        [msg, msg, fine, wins, wins],
        [sums, rims, wins, (8, 128), wins, halves, (2, PLANES * ROWS, 128)],
        partial, xa, xb, ya, yb, other, coef, agg, s_win,
    )
    mb = swap(mb, "sy", 1)
    ma = swap(ma, "sy")
    residual, r_win = call(
        store_kernel, [fine, wins], [], residual, r_win, out_space=[HBM, VMEM], sems=1
    )
    face = (EDGE_ROWS * GROUP, CZ)
    db, da, delta, r_win = call(
        first_kernel, [face, face, wins, wins], [], r_win, s_win, ma, mb
    )
    db = swap(db, "sx", 1)
    da = swap(da, "sx")
    other_delta = swap(delta, "hb")
    (step,) = call(second_kernel, [wins], [], mixing, r_win, s_win, delta, spaces=[SMEM])
    (corrected,) = call(
        final_kernel,
        [fine],
        [wins, (2,) + wins, (2,) + wins, (2,) + wins, (2, GROUP * ROWS, CZ), fine],
        step, da, db, other_delta, state, agg,
        out_space=HBM,
        sems=HERE,
    )
    return corrected.reshape(shape), residual.reshape(shape)


def solution(mesh):
    whole = P("hb", None, "sx", "sy", None)
    return jax.shard_map(
        shards,
        mesh=mesh,
        in_specs=(whole, whole, P("sx", "sy", None), P(), P("sx", "sy", None)),
        out_specs=(whole, whole),
        check_vma=False,
    )
```

time: 67.2 us -> 59.8 us (0.89)
  the two profiles are of different devices: /device:TPU:62 before, /device:TPU:254 now
where the time goes in v2:
time: 59.8 us; the launch traced here: 59.4 us
  starting transfers between devices  33.6 us (56%)
  waiting for transfers between devices  19.1 us (32%)
  Pallas kernels  5.88 us (10%)
  between operations  0.79 us (1%)
    ppermute x10, starting transfers between devices, swap(): return lax.ppermute(value, axis, swap_pairs(axis, first))  33.6 us
    ppermute x10, waiting for transfers between devices, swap(): return lax.ppermute(value, axis, swap_pairs(axis, first))  19.1 us
    pallas_call x7, Pallas kernels, call(): pl.pallas_call(kernel, out_shape=outs, in_specs=spaces, out_specs=out_spa...  5.88 us
  transfers between devices with their start and end apart: 10, of which 4 were waited for; matrix products, arithmetic and copies ran while one was open for 0% of the time, Pallas kernels for 5%

profile of v2, /device:TPU:254, one launch (start us, length us, event | category | flops | bytes accessed | tf_op | source)
XLA Modules:
  0.0 59.4 jit_solution(15000940805522181509)
XLA Ops:
  0.6 1.4 %edges_kernel.1 = (f32[96,256]{1,0:T(8,128)S(1)}, f32[120,256]{1,0:T(8,128)S(1)}, f32[120,256]{1,0:T(8,128)S(1)}, f32[96,256]{1,0:T(8,128)S(1)}, f32[480,256]{1,...) custom-call(f32[480,256]{1,0:T(8,128)} %bitcast.6, ...), custom_call_target="tpu_custom_call" | custom-call | tf_op jit(solution)/shard_map/edges_kernel/pallas_call | solution.py:374
  2.0 1.9 %collective-permute-start.4 = (f32[480,256]{1,0:T(8,128)S(1)}, f32[480,256]{1,0:T(8,128)S(1)}, u32[]{:S(2)}, u32[]{:S(2)}) collective-permute-start(f32[480,256]{1,0:T(8,128)S(1)} %get-tuple-element.22.state), channel_id=1, source_target_pairs={{0,1},{1,0},{2,3},{3,2},{4,5},{5,4},{6,7},{7,6},{8,9},{9,8},{10,11... | collective-permute-start | bytes 1474568 | tf_op jit(solution)/shard_map/ppermute | solution.py:402
  4.0 2.7 %collective-permute-start = (f32[120,256]{1,0:T(8,128)S(1)}, f32[120,256]{1,0:T(8,128)S(1)}, u32[]{:S(2)}, u32[]{:S(2)}) collective-permute-start(f32[120,256]{1,0:T(8,128)S(1)} %get-tuple-element.25), channel_id=1, source_target_pairs={{0,64},{128,192},{256,320},{384,448},{512,576},{640,704},{64,0},{1... | collective-permute-start | bytes 368648 | tf_op jit(solution)/shard_map/ppermute | solution.py:402
  6.7 0.0 copy-start
  6.7 6.1 %collective-permute-start.1 = (f32[120,256]{1,0:T(8,128)S(1)}, f32[120,256]{1,0:T(8,128)S(1)}, u32[]{:S(2)}, u32[]{:S(2)}) collective-permute-start(f32[120,256]{1,0:T(8,128)S(1)} %get-tuple-element.26), channel_id=1, source_target_pairs={{64,128},{192,256},{320,384},{448,512},{576,640},{128,64},{256,192... | collective-permute-start | bytes 368648 | tf_op jit(solution)/shard_map/ppermute | solution.py:402
  12.8 3.3 %collective-permute-start.2 = (f32[96,256]{1,0:T(8,128)S(1)}, f32[96,256]{1,0:T(8,128)S(1)}, u32[]{:S(2)}, u32[]{:S(2)}) collective-permute-start(f32[96,256]{1,0:T(8,128)S(1)} %get-tuple-element.27), channel_id=1, source_target_pairs={{0,2},{4,6},{8,10},{12,14},{16,18},{20,22},{24,26},{28,30},{32,34}... | collective-permute-start | bytes 294920 | tf_op jit(solution)/shard_map/ppermute | solution.py:402
  16.1 7.0 %collective-permute-start.3 = (f32[96,256]{1,0:T(8,128)S(1)}, f32[96,256]{1,0:T(8,128)S(1)}, u32[]{:S(2)}, u32[]{:S(2)}) collective-permute-start(f32[96,256]{1,0:T(8,128)S(1)} %get-tuple-element.28), channel_id=1, source_target_pairs={{2,4},{6,8},{10,12},{14,16},{18,20},{22,24},{26,28},{30,32},{34,36... | collective-permute-start | bytes 294920 | tf_op jit(solution)/shard_map/ppermute | solution.py:402
  23.1 0.0 copy-done
  23.1 1.1 %inner_kernel.1.partial = f32[480,256]{1,0:T(8,128)S(1)} custom-call(f32[5,5]{1,0:T(8,128)S(1)} %copy-done, f32[480,256]{1,0:T(8,128)S(1)} %get-tuple-element.22.state, f32[480,256]{1,0:T(8,128)S(1)} %get-tuple-element.23.forcing, f32[32,256]{1,0:T(8,128)S(1)} %get-tuple-element.24.coef), custom_call_target="tpu_custom_call" | custom-call | tf_op jit(solution)/shard_map/inner_kernel/pallas_call | solution.py:374
  24.3 0.0 collective-permute-done.2.ya
  24.3 7.1 %collective-permute-done.3.yb = f32[96,256]{1,0:T(8,128)S(1)} collective-permute-done((f32[96,256]{1,0:T(8,128)S(1)}, f32[96,256]{1,0:T(8,128)S(1)}, u32[]{:S(2)}, u32[]{:S(2)}) %collective-permute-start.3) | collective-permute-done | bytes 98336 | tf_op jit(solution)/shard_map/ppermute | solution.py:402
  31.3 0.0 collective-permute-done.xa
  31.3 0.0 collective-permute-done.1.xb
  31.3 0.0 collective-permute-done.4.other
  31.4 0.5 outer_kernel.1
  31.9 1.9 %collective-permute-start.5 = (f32[96,128]{1,0:T(8,128)S(1)}, f32[96,128]{1,0:T(8,128)S(1)}, u32[]{:S(2)}, u32[]{:S(2)}) collective-permute-start(f32[96,128]{1,0:T(8,128)S(1)} %get-tuple-element.35), channel_id=1, source_target_pairs={{0,2},{4,6},{8,10},{12,14},{16,18},{20,22},{24,26},{28,30},{32,34}... | collective-permute-start | bytes 147464 | tf_op jit(solution)/shard_map/ppermute | solution.py:402
  33.8 4.9 %collective-permute-start.6 = (f32[96,128]{1,0:T(8,128)S(1)}, f32[96,128]{1,0:T(8,128)S(1)}, u32[]{:S(2)}, u32[]{:S(2)}) collective-permute-start(f32[96,128]{1,0:T(8,128)S(1)} %get-tuple-element.36), channel_id=1, source_target_pairs={{2,4},{6,8},{10,12},{14,16},{18,20},{22,24},{26,28},{30,32},{34,36... | collective-permute-start | bytes 147464 | tf_op jit(solution)/shard_map/ppermute | solution.py:402
  38.7 0.8 %store_kernel.1 = (f32[480,256]{1,0:T(8,128)}, f32[256,128]{1,0:T(8,128)S(1)}) custom-call(f32[480,256]{1,0:T(8,128)S(1)} %get-tuple-element.31.values, f32[256,128]{1,0:T(8,128)S(1)} %get-tuple-element.32.r_in), custom_call_target="tpu_custom_call" | custom-call | tf_op jit(solution)/shard_map/store_kernel/pallas_call | solution.py:374
  39.5 0.0 collective-permute-done.5.ma
  39.5 5.4 %collective-permute-done.6.mb = f32[96,128]{1,0:T(8,128)S(1)} collective-permute-done((f32[96,128]{1,0:T(8,128)S(1)}, f32[96,128]{1,0:T(8,128)S(1)}, u32[]{:S(2)}, u32[]{:S(2)}) %collective-permute-start.6) | collective-permute-done | bytes 49184 | tf_op jit(solution)/shard_map/ppermute | solution.py:402
  44.9 0.1 first_kernel.1
  45.0 1.9 %collective-permute-start.9 = (f32[256,128]{1,0:T(8,128)S(1)}, f32[256,128]{1,0:T(8,128)S(1)}, u32[]{:S(2)}, u32[]{:S(2)}) collective-permute-start(f32[256,128]{1,0:T(8,128)S(1)} %get-tuple-element.38.delta), channel_id=1, source_target_pairs={{0,1},{1,0},{2,3},{3,2},{4,5},{5,4},{6,7},{7,6},{8,9},{9,8},{10,11... | collective-permute-start | bytes 393224 | tf_op jit(solution)/shard_map/ppermute | solution.py:402
  46.9 1.9 %collective-permute-start.7 = (f32[96,128]{1,0:T(8,128)S(1)}, f32[96,128]{1,0:T(8,128)S(1)}, u32[]{:S(2)}, u32[]{:S(2)}) collective-permute-start(f32[96,128]{1,0:T(8,128)S(1)} %get-tuple-element.39), channel_id=1, source_target_pairs={{0,64},{128,192},{256,320},{384,448},{512,576},{640,704},{64,0},{1... | collective-permute-start | bytes 147464 | tf_op jit(solution)/shard_map/ppermute | solution.py:402
  48.9 1.9 %collective-permute-start.8 = (f32[96,128]{1,0:T(8,128)S(1)}, f32[96,128]{1,0:T(8,128)S(1)}, u32[]{:S(2)}, u32[]{:S(2)}) collective-permute-start(f32[96,128]{1,0:T(8,128)S(1)} %get-tuple-element.40), channel_id=1, source_target_pairs={{64,128},{192,256},{320,384},{448,512},{576,640},{128,64},{256,192... | collective-permute-start | bytes 147464 | tf_op jit(solution)/shard_map/ppermute | solution.py:402
  50.8 0.8 %second_kernel.1.partial = f32[256,128]{1,0:T(8,128)S(1)} custom-call(f32[5,5]{1,0:T(8,128)S(1)} %copy-done, f32[256,128]{1,0:T(8,128)S(1)} %get-tuple-element.37.r_win, f32[256,128]{1,0:T(8,128)S(1)} %get-tuple-element.34.s_win, f32[256,128]{1,0:T(8,128)S(1)} %get-tuple-element.38.delta), custom_call_target="tpu_custom_call" | custom-call | tf_op jit(solution)/shard_map/second_kernel/pallas_call | solution.py:374
  51.6 1.4 %collective-permute-done.7.xa = f32[96,128]{1,0:T(8,128)S(1)} collective-permute-done((f32[96,128]{1,0:T(8,128)S(1)}, f32[96,128]{1,0:T(8,128)S(1)}, u32[]{:S(2)}, u32[]{:S(2)}) %collective-permute-start.7) | collective-permute-done | bytes 49184 | tf_op jit(solution)/shard_map/ppermute | solution.py:402
  53.0 5.2 %collective-permute-done.8.xb = f32[96,128]{1,0:T(8,128)S(1)} collective-permute-done((f32[96,128]{1,0:T(8,128)S(1)}, f32[96,128]{1,0:T(8,128)S(1)}, u32[]{:S(2)}, u32[]{:S(2)}) %collective-permute-start.8) | collective-permute-done | bytes 49184 | tf_op jit(solution)/shard_map/ppermute | solution.py:402
  58.2 0.0 collective-permute-done.9.other
  58.2 1.1 %final_kernel.1 = f32[480,256]{1,0:T(8,128)} custom-call(f32[256,128]{1,0:T(8,128)S(1)} %second_kernel.1.partial, f32[96,128]{1,0:T(8,128)S(1)} %collective-permute-done.7.xa, f32[96,128]{1,0:T(8,128)S(1)} %collective-permute-done.8.xb, f32[256,128]{1,0:T(8,128)S(1)} %collective-permute-done.9.other, f32[480,256]{1,0:T(8,128)S(1)} %get-tuple-element.22.state, ...), custom_call_target="tpu_custom_call" | custom-call | tf_op jit(solution)/shard_map/final_kernel/pallas_call | solution.py:374
Async XLA Ops:
  2.0 29.3 %collective-permute-start.4 = (f32[480,256]{1,0:T(8,128)S(1)}, f32[480,256]{1,0:T(8,128)S(1)}, u32[]{:S(2)}, u32[]{:S(2)}) collective-permute-start(f32[480,256]{1,0:T(8,128)S(1)} %get-tuple-element.22.state), channel_id=1, source_target_pairs={{0,1},{1,0},{2,3},{3,2},{4,5},{5,4},{6,7},{7,6},{8,9},{9,8},{10,11... | collective-permute-start | bytes 1474568 | tf_op jit(solution)/shard_map/ppermute | solution.py:402
  4.0 27.4 %collective-permute-start = (f32[120,256]{1,0:T(8,128)S(1)}, f32[120,256]{1,0:T(8,128)S(1)}, u32[]{:S(2)}, u32[]{:S(2)}) collective-permute-start(f32[120,256]{1,0:T(8,128)S(1)} %get-tuple-element.25), channel_id=1, source_target_pairs={{0,64},{128,192},{256,320},{384,448},{512,576},{640,704},{64,0},{1... | collective-permute-start | bytes 368648 | tf_op jit(solution)/shard_map/ppermute | solution.py:402
  6.7 16.4 %copy-start = (f32[5,5]{1,0:T(8,128)S(1)}, f32[5,5]{1,0:T(8,128)}, u32[]{:S(2)}) copy-start(f32[5,5]{1,0:T(8,128)} %mixing.3) | copy-start | bytes 304
  6.7 24.6 %collective-permute-start.1 = (f32[120,256]{1,0:T(8,128)S(1)}, f32[120,256]{1,0:T(8,128)S(1)}, u32[]{:S(2)}, u32[]{:S(2)}) collective-permute-start(f32[120,256]{1,0:T(8,128)S(1)} %get-tuple-element.26), channel_id=1, source_target_pairs={{64,128},{192,256},{320,384},{448,512},{576,640},{128,64},{256,192... | collective-permute-start | bytes 368648 | tf_op jit(solution)/shard_map/ppermute | solution.py:402
  12.8 11.5 %collective-permute-start.2 = (f32[96,256]{1,0:T(8,128)S(1)}, f32[96,256]{1,0:T(8,128)S(1)}, u32[]{:S(2)}, u32[]{:S(2)}) collective-permute-start(f32[96,256]{1,0:T(8,128)S(1)} %get-tuple-element.27), channel_id=1, source_target_pairs={{0,2},{4,6},{8,10},{12,14},{16,18},{20,22},{24,26},{28,30},{32,34}... | collective-permute-start | bytes 294920 | tf_op jit(solution)/shard_map/ppermute | solution.py:402
  16.1 15.3 %collective-permute-start.3 = (f32[96,256]{1,0:T(8,128)S(1)}, f32[96,256]{1,0:T(8,128)S(1)}, u32[]{:S(2)}, u32[]{:S(2)}) collective-permute-start(f32[96,256]{1,0:T(8,128)S(1)} %get-tuple-element.28), channel_id=1, source_target_pairs={{2,4},{6,8},{10,12},{14,16},{18,20},{22,24},{26,28},{30,32},{34,36... | collective-permute-start | bytes 294920 | tf_op jit(solution)/shard_map/ppermute | solution.py:402
  31.9 7.6 %collective-permute-start.5 = (f32[96,128]{1,0:T(8,128)S(1)}, f32[96,128]{1,0:T(8,128)S(1)}, u32[]{:S(2)}, u32[]{:S(2)}) collective-permute-start(f32[96,128]{1,0:T(8,128)S(1)} %get-tuple-element.35), channel_id=1, source_target_pairs={{0,2},{4,6},{8,10},{12,14},{16,18},{20,22},{24,26},{28,30},{32,34}... | collective-permute-start | bytes 147464 | tf_op jit(solution)/shard_map/ppermute | solution.py:402
  33.8 11.1 %collective-permute-start.6 = (f32[96,128]{1,0:T(8,128)S(1)}, f32[96,128]{1,0:T(8,128)S(1)}, u32[]{:S(2)}, u32[]{:S(2)}) collective-permute-start(f32[96,128]{1,0:T(8,128)S(1)} %get-tuple-element.36), channel_id=1, source_target_pairs={{2,4},{6,8},{10,12},{14,16},{18,20},{22,24},{26,28},{30,32},{34,36... | collective-permute-start | bytes 147464 | tf_op jit(solution)/shard_map/ppermute | solution.py:402
  45.0 13.2 %collective-permute-start.9 = (f32[256,128]{1,0:T(8,128)S(1)}, f32[256,128]{1,0:T(8,128)S(1)}, u32[]{:S(2)}, u32[]{:S(2)}) collective-permute-start(f32[256,128]{1,0:T(8,128)S(1)} %get-tuple-element.38.delta), channel_id=1, source_target_pairs={{0,1},{1,0},{2,3},{3,2},{4,5},{5,4},{6,7},{7,6},{8,9},{9,8},{10,11... | collective-permute-start | bytes 393224 | tf_op jit(solution)/shard_map/ppermute | solution.py:402
  46.9 6.0 %collective-permute-start.7 = (f32[96,128]{1,0:T(8,128)S(1)}, f32[96,128]{1,0:T(8,128)S(1)}, u32[]{:S(2)}, u32[]{:S(2)}) collective-permute-start(f32[96,128]{1,0:T(8,128)S(1)} %get-tuple-element.39), channel_id=1, source_target_pairs={{0,64},{128,192},{256,320},{384,448},{512,576},{640,704},{64,0},{1... | collective-permute-start | bytes 147464 | tf_op jit(solution)/shard_map/ppermute | solution.py:402
  48.9 9.4 %collective-permute-start.8 = (f32[96,128]{1,0:T(8,128)S(1)}, f32[96,128]{1,0:T(8,128)S(1)}, u32[]{:S(2)}, u32[]{:S(2)}) collective-permute-start(f32[96,128]{1,0:T(8,128)S(1)} %get-tuple-element.40), channel_id=1, source_target_pairs={{64,128},{192,256},{320,384},{448,512},{576,640},{128,64},{256,192... | collective-permute-start | bytes 147464 | tf_op jit(solution)/shard_map/ppermute | solution.py:402

commit v3 on v2

--- a/solution.py
+++ b/solution.py
@@ -196,10 +196,11 @@
 
 
 def outer_kernel(
-    partial, xa, xb, ya, yb, other, coef, agg, s_in,
+    partial, yb, ya, xb, xa, other, coef, agg, s_in,
     mb, ma, residual, r_win, s_win, sums, rims, summed, edge, scaled, halves, coefs,
 ):
     even_x, even_y = (even_index("sx"), even_index("sy"))
+    peer = 1 - lax.axis_index("hb")
     for x in range(PLANES):
         c = coef[pl.ds(x * ROWS, ROWS), :]
         for i in range(HERE):
@@ -208,7 +209,7 @@
                 face = pl.ds(field * ROWS, ROWS)
                 total = partial[tile(field, x), :]
                 for j in range(HERE):
-                    total = total - OTHER[i][j] * other[tile(j * VARS + v, x), :]
+                    total = total - OTHER[i][j] * other[peer, tile(j * VARS + v, x), :]
                 if x == 0:
                     total = total + c * choose(even_x, xb[face, :], xa[face, :])
                 if x == PLANES - 1:
@@ -257,7 +258,7 @@
 EDGE_ROWS = 6
 
 
-def first_kernel(r_in, s_win, ma, mb, xb, xa, delta, r_win):
+def first_kernel(r_in, s_win, mb, ma, xb, xa, delta, r_win):
     even_x, even_y = (even_index("sx"), even_index("sy"))
     r_win[...] = r_in[...]
     pieces = []
@@ -307,9 +308,10 @@
 
 
 def final_kernel(
-    partial, xa, xb, other, state, agg, corrected, change, fine, own, beside, halos, result, sems
+    partial, xb, xa, other, state, agg, corrected, change, fine, own, beside, halos, result, sems
 ):
     even_x = even_index("sx")
+    peer = 1 - lax.axis_index("hb")
     for r in range(EDGE_ROWS):
         at_a, at_b = (xa[pl.ds(r * GROUP, GROUP), :], xb[pl.ds(r * GROUP, GROUP), :])
         rows = pl.ds(r + 1, GROUP, stride=ROWS)
@@ -326,7 +328,7 @@
                 field = i * VARS + v
                 total = coef_c * halos[p, pl.ds(field * ROWS, ROWS), :]
                 for j in range(HERE):
-                    total = total - OTHER[i][j] * other[window(p, j * VARS + v), :]
+                    total = total - OTHER[i][j] * other[peer, window(p, j * VARS + v), :]
                 change[window(p, field), :] = partial[window(p, field), :] + scale * total
         change[window(p, FIELDS), :] = jnp.zeros((ROWS, CZ), F32)
     twice = (iota((CZ, NZ), 1) >> 1 == iota((CZ, NZ), 0)).astype(BF16)
@@ -405,7 +407,7 @@
     sums = (WIN * ROWS, NZ)
     rims = (2, WIN * ROWS, 128)
     x_face = (FIELDS * ROWS, NZ)
-    y_face = (64 + WIN, NZ)
+    y_face = (120, NZ)
     yb, xb, xa, ya, state, forcing, coef, agg, s_win = call(
         edges_kernel,
         [y_face, x_face, x_face, y_face, fine, fine, coef.shape, agg, wins],
@@ -418,14 +420,14 @@
     xb = swap(xb, "sx", 1)
     xa = swap(xa, "sx")
     ya = swap(ya, "sy")
-    other = swap(state, "hb")
+    other = lax.all_gather(state, "hb")
     (partial,) = call(inner_kernel, [fine], [], mixing, state, forcing, coef, spaces=[SMEM])
     msg = (3 * WIN, CZ)
     mb, ma, residual, r_win, s_win = call(
         outer_kernel,
         [msg, msg, fine, wins, wins],
         [sums, rims, wins, (8, 128), wins, halves, (2, PLANES * ROWS, 128)],
-        partial, xa, xb, ya, yb, other, coef, agg, s_win,
+        partial, yb, ya, xb, xa, other, coef, agg, s_win,
     )
     mb = swap(mb, "sy", 1)
     ma = swap(ma, "sy")
@@ -434,17 +436,17 @@
     )
     face = (EDGE_ROWS * GROUP, CZ)
     db, da, delta, r_win = call(
-        first_kernel, [face, face, wins, wins], [], r_win, s_win, ma, mb
+        first_kernel, [face, face, wins, wins], [], r_win, s_win, mb, ma
     )
     db = swap(db, "sx", 1)
     da = swap(da, "sx")
-    other_delta = swap(delta, "hb")
+    other_delta = lax.all_gather(delta, "hb")
     (step,) = call(second_kernel, [wins], [], mixing, r_win, s_win, delta, spaces=[SMEM])
     (corrected,) = call(
         final_kernel,
         [fine],
         [wins, (2,) + wins, (2,) + wins, (2,) + wins, (2, GROUP * ROWS, CZ), fine],
-        step, da, db, other_delta, state, agg,
+        step, db, da, other_delta, state, agg,
         out_space=HBM,
         sems=HERE,
     )

time: 59.8 us -> 48.6 us (0.81)
  the two profiles are of different devices: /device:TPU:254 before, /device:TPU:253 now
where the time goes in v3:
time: 48.6 us; the launch traced here: 48.2 us
  starting transfers between devices  26.9 us (55%)
  blocking collectives  9.62 us (20%)
  Pallas kernels  5.89 us (12%)
  waiting for transfers between devices  5.01 us (10%)
  between operations  0.78 us (2%)
    ppermute x8, starting transfers between devices, swap(): return lax.ppermute(value, axis, swap_pairs(axis, first))  26.9 us
    all_gather x1, blocking collectives, shards(): other_delta = lax.all_gather(delta, 'hb')  5.97 us
    pallas_call x7, Pallas kernels, call(): pl.pallas_call(kernel, out_shape=outs, in_specs=spaces, out_specs=out_spa...  5.89 us
    ppermute x8, waiting for transfers between devices, swap(): return lax.ppermute(value, axis, swap_pairs(axis, first))  5.01 us
    all_gather x1, blocking collectives, shards(): other = lax.all_gather(state, 'hb')  3.65 us
  transfers between devices with their start and end apart: 8, of which 1 were waited for; matrix products, arithmetic and copies ran while one was open for 0% of the time, Pallas kernels for 6%

profile of v3, /device:TPU:253, one launch (start us, length us, event | category | flops | bytes accessed | tf_op | source)
XLA Modules:
  0.0 48.2 jit_solution(7673912187766559775)
XLA Ops:
  0.6 1.4 %edges_kernel.1 = (f32[120,256]{1,0:T(8,128)S(1)}, f32[120,256]{1,0:T(8,128)S(1)}, f32[120,256]{1,0:T(8,128)S(1)}, f32[120,256]{1,0:T(8,128)S(1)}, f32[480,256]{...) custom-call(f32[480,256]{1,0:T(8,128)} %bitcast.10, ...), custom_call_target="tpu_custom_call" | custom-call | tf_op jit(solution)/shard_map/edges_kernel/pallas_call | solution.py:376
  2.0 8.0 %collective-permute-start = (f32[120,256]{1,0:T(8,128)S(1)}, f32[120,256]{1,0:T(8,128)S(1)}, u32[]{:S(2)}, u32[]{:S(2)}) collective-permute-start(f32[120,256]{1,0:T(8,128)S(1)} %get-tuple-element.25), channel_id=1, source_target_pairs={{2,4},{6,8},{10,12},{14,16},{18,20},{22,24},{26,28},{30,32},{34,36... | collective-permute-start | bytes 368648 | tf_op jit(solution)/shard_map/ppermute | solution.py:404
  10.1 1.9 %collective-permute-start.1 = (f32[120,256]{1,0:T(8,128)S(1)}, f32[120,256]{1,0:T(8,128)S(1)}, u32[]{:S(2)}, u32[]{:S(2)}) collective-permute-start(f32[120,256]{1,0:T(8,128)S(1)} %get-tuple-element.26), channel_id=1, source_target_pairs={{0,2},{4,6},{8,10},{12,14},{16,18},{20,22},{24,26},{28,30},{32,34}... | collective-permute-start | bytes 368648 | tf_op jit(solution)/shard_map/ppermute | solution.py:404
  12.0 2.2 %collective-permute-start.2 = (f32[120,256]{1,0:T(8,128)S(1)}, f32[120,256]{1,0:T(8,128)S(1)}, u32[]{:S(2)}, u32[]{:S(2)}) collective-permute-start(f32[120,256]{1,0:T(8,128)S(1)} %get-tuple-element.27), channel_id=1, source_target_pairs={{64,128},{192,256},{320,384},{448,512},{576,640},{128,64},{256,192... | collective-permute-start | bytes 368648 | tf_op jit(solution)/shard_map/ppermute | solution.py:404
  14.2 4.3 %collective-permute-start.3 = (f32[120,256]{1,0:T(8,128)S(1)}, f32[120,256]{1,0:T(8,128)S(1)}, u32[]{:S(2)}, u32[]{:S(2)}) collective-permute-start(f32[120,256]{1,0:T(8,128)S(1)} %get-tuple-element.28), channel_id=1, source_target_pairs={{0,64},{128,192},{256,320},{384,448},{512,576},{640,704},{64,0},{1... | collective-permute-start | bytes 368648 | tf_op jit(solution)/shard_map/ppermute | solution.py:404
  18.5 0.0 copy-start
  18.5 3.7 %all-gather = f32[960,256]{1,0:T(8,128)S(1)} all-gather(f32[480,256]{1,0:T(8,128)S(1)} %get-tuple-element.22.state), channel_id=2, replica_groups=mesh['sx'=12,'sy'=32,'hb'=2] {'hb'}, dimensions={0}, use_global_device_ids=true | all-gather | bytes 1474560 | tf_op jit(solution)/shard_map/all_gather | solution.py:423
  22.1 0.0 copy-done
  22.1 1.1 %inner_kernel.1.partial = f32[480,256]{1,0:T(8,128)S(1)} custom-call(f32[5,5]{1,0:T(8,128)S(1)} %copy-done, f32[480,256]{1,0:T(8,128)S(1)} %get-tuple-element.22.state, f32[480,256]{1,0:T(8,128)S(1)} %get-tuple-element.23.forcing, f32[32,256]{1,0:T(8,128)S(1)} %get-tuple-element.24.coef), custom_call_target="tpu_custom_call" | custom-call | tf_op jit(solution)/shard_map/inner_kernel/pallas_call | solution.py:376
  23.3 0.0 collective-permute-done.yb
  23.3 0.0 collective-permute-done.1.ya
  23.3 0.0 collective-permute-done.2.xb
  23.3 0.0 collective-permute-done.3.xa
  23.3 0.5 %outer_kernel.1 = (f32[96,128]{1,0:T(8,128)S(1)}, f32[96,128]{1,0:T(8,128)S(1)}, f32[480,256]{1,0:T(8,128)S(1)}, f32[256,128]{1,0:T(8,128)S(1)}, f32[256,128]{1,0:T(8,128)S(1)}) custom-call(f32[480,256]{1,0:T(8,128)S(1)} %inner_kernel.1.partial, f32[120,256]{1,0:T(8,128)S(1)} %collective-permute-done.yb, f32[120,256]{1,0:T(8,128)S(1)} %collective-permute-done.1.ya, ...), custom_call_target="tpu_custom_call" | custom-call | tf_op jit(solution)/shard_map/outer_kernel/pallas_call | solution.py:376
  23.9 4.8 %collective-permute-start.4 = (f32[96,128]{1,0:T(8,128)S(1)}, f32[96,128]{1,0:T(8,128)S(1)}, u32[]{:S(2)}, u32[]{:S(2)}) collective-permute-start(f32[96,128]{1,0:T(8,128)S(1)} %get-tuple-element.35), channel_id=1, source_target_pairs={{2,4},{6,8},{10,12},{14,16},{18,20},{22,24},{26,28},{30,32},{34,36... | collective-permute-start | bytes 147464 | tf_op jit(solution)/shard_map/ppermute | solution.py:404
  28.6 1.9 %collective-permute-start.5 = (f32[96,128]{1,0:T(8,128)S(1)}, f32[96,128]{1,0:T(8,128)S(1)}, u32[]{:S(2)}, u32[]{:S(2)}) collective-permute-start(f32[96,128]{1,0:T(8,128)S(1)} %get-tuple-element.36), channel_id=1, source_target_pairs={{0,2},{4,6},{8,10},{12,14},{16,18},{20,22},{24,26},{28,30},{32,34}... | collective-permute-start | bytes 147464 | tf_op jit(solution)/shard_map/ppermute | solution.py:404
  30.6 0.8 %store_kernel.1 = (f32[480,256]{1,0:T(8,128)}, f32[256,128]{1,0:T(8,128)S(1)}) custom-call(f32[480,256]{1,0:T(8,128)S(1)} %get-tuple-element.31.values, f32[256,128]{1,0:T(8,128)S(1)} %get-tuple-element.32.r_in), custom_call_target="tpu_custom_call" | custom-call | tf_op jit(solution)/shard_map/store_kernel/pallas_call | solution.py:376
  31.4 5.0 %collective-permute-done.4.mb = f32[96,128]{1,0:T(8,128)S(1)} collective-permute-done((f32[96,128]{1,0:T(8,128)S(1)}, f32[96,128]{1,0:T(8,128)S(1)}, u32[]{:S(2)}, u32[]{:S(2)}) %collective-permute-start.4) | collective-permute-done | bytes 49184 | tf_op jit(solution)/shard_map/ppermute | solution.py:404
  36.4 0.0 collective-permute-done.5.ma
  36.4 0.1 first_kernel.1
  36.5 1.9 %collective-permute-start.6 = (f32[96,128]{1,0:T(8,128)S(1)}, f32[96,128]{1,0:T(8,128)S(1)}, u32[]{:S(2)}, u32[]{:S(2)}) collective-permute-start(f32[96,128]{1,0:T(8,128)S(1)} %get-tuple-element.39), channel_id=1, source_target_pairs={{64,128},{192,256},{320,384},{448,512},{576,640},{128,64},{256,192... | collective-permute-start | bytes 147464 | tf_op jit(solution)/shard_map/ppermute | solution.py:404
  38.4 1.9 %collective-permute-start.7 = (f32[96,128]{1,0:T(8,128)S(1)}, f32[96,128]{1,0:T(8,128)S(1)}, u32[]{:S(2)}, u32[]{:S(2)}) collective-permute-start(f32[96,128]{1,0:T(8,128)S(1)} %get-tuple-element.40), channel_id=1, source_target_pairs={{0,64},{128,192},{256,320},{384,448},{512,576},{640,704},{64,0},{1... | collective-permute-start | bytes 147464 | tf_op jit(solution)/shard_map/ppermute | solution.py:404
  40.3 0.8 %second_kernel.1.partial = f32[256,128]{1,0:T(8,128)S(1)} custom-call(f32[5,5]{1,0:T(8,128)S(1)} %copy-done, f32[256,128]{1,0:T(8,128)S(1)} %get-tuple-element.37.r_win, f32[256,128]{1,0:T(8,128)S(1)} %get-tuple-element.34.s_win, f32[256,128]{1,0:T(8,128)S(1)} %get-tuple-element.38.delta), custom_call_target="tpu_custom_call" | custom-call | tf_op jit(solution)/shard_map/second_kernel/pallas_call | solution.py:376
  41.1 6.0 %all-gather.1 = f32[512,128]{1,0:T(8,128)S(1)} all-gather(f32[256,128]{1,0:T(8,128)S(1)} %get-tuple-element.38.delta), channel_id=3, replica_groups=mesh['sx'=12,'sy'=32,'hb'=2] {'hb'}, dimensions={0}, use_global_device_ids=true | all-gather | bytes 393216 | tf_op jit(solution)/shard_map/all_gather | solution.py:443
  47.1 0.0 collective-permute-done.6.xb
  47.1 0.0 collective-permute-done.7.xa
  47.1 1.2 %final_kernel.1 = f32[480,256]{1,0:T(8,128)} custom-call(f32[256,128]{1,0:T(8,128)S(1)} %second_kernel.1.partial, f32[96,128]{1,0:T(8,128)S(1)} %collective-permute-done.6.xb, f32[96,128]{1,0:T(8,128)S(1)} %collective-permute-done.7.xa, f32[2,256,128]{2,1,0:T(8,128)S(1)} %bitcast.9, f32[480,256]{1,0:T(8,128)S(1)} %get-tuple-element.22.state, ...), custom_call_target="tpu_custom_call" | custom-call | tf_op jit(solution)/shard_map/final_kernel/pallas_call | solution.py:376
Async XLA Ops:
  2.0 21.3 %collective-permute-start = (f32[120,256]{1,0:T(8,128)S(1)}, f32[120,256]{1,0:T(8,128)S(1)}, u32[]{:S(2)}, u32[]{:S(2)}) collective-permute-start(f32[120,256]{1,0:T(8,128)S(1)} %get-tuple-element.25), channel_id=1, source_target_pairs={{2,4},{6,8},{10,12},{14,16},{18,20},{22,24},{26,28},{30,32},{34,36... | collective-permute-start | bytes 368648 | tf_op jit(solution)/shard_map/ppermute | solution.py:404
  10.1 13.2 %collective-permute-start.1 = (f32[120,256]{1,0:T(8,128)S(1)}, f32[120,256]{1,0:T(8,128)S(1)}, u32[]{:S(2)}, u32[]{:S(2)}) collective-permute-start(f32[120,256]{1,0:T(8,128)S(1)} %get-tuple-element.26), channel_id=1, source_target_pairs={{0,2},{4,6},{8,10},{12,14},{16,18},{20,22},{24,26},{28,30},{32,34}... | collective-permute-start | bytes 368648 | tf_op jit(solution)/shard_map/ppermute | solution.py:404
  12.0 11.3 %collective-permute-start.2 = (f32[120,256]{1,0:T(8,128)S(1)}, f32[120,256]{1,0:T(8,128)S(1)}, u32[]{:S(2)}, u32[]{:S(2)}) collective-permute-start(f32[120,256]{1,0:T(8,128)S(1)} %get-tuple-element.27), channel_id=1, source_target_pairs={{64,128},{192,256},{320,384},{448,512},{576,640},{128,64},{256,192... | collective-permute-start | bytes 368648 | tf_op jit(solution)/shard_map/ppermute | solution.py:404
  14.2 9.1 %collective-permute-start.3 = (f32[120,256]{1,0:T(8,128)S(1)}, f32[120,256]{1,0:T(8,128)S(1)}, u32[]{:S(2)}, u32[]{:S(2)}) collective-permute-start(f32[120,256]{1,0:T(8,128)S(1)} %get-tuple-element.28), channel_id=1, source_target_pairs={{0,64},{128,192},{256,320},{384,448},{512,576},{640,704},{64,0},{1... | collective-permute-start | bytes 368648 | tf_op jit(solution)/shard_map/ppermute | solution.py:404
  18.5 3.7 %copy-start = (f32[5,5]{1,0:T(8,128)S(1)}, f32[5,5]{1,0:T(8,128)}, u32[]{:S(2)}) copy-start(f32[5,5]{1,0:T(8,128)} %mixing.3) | copy-start | bytes 304
  23.9 12.5 %collective-permute-start.4 = (f32[96,128]{1,0:T(8,128)S(1)}, f32[96,128]{1,0:T(8,128)S(1)}, u32[]{:S(2)}, u32[]{:S(2)}) collective-permute-start(f32[96,128]{1,0:T(8,128)S(1)} %get-tuple-element.35), channel_id=1, source_target_pairs={{2,4},{6,8},{10,12},{14,16},{18,20},{22,24},{26,28},{30,32},{34,36... | collective-permute-start | bytes 147464 | tf_op jit(solution)/shard_map/ppermute | solution.py:404
  28.6 7.7 %collective-permute-start.5 = (f32[96,128]{1,0:T(8,128)S(1)}, f32[96,128]{1,0:T(8,128)S(1)}, u32[]{:S(2)}, u32[]{:S(2)}) collective-permute-start(f32[96,128]{1,0:T(8,128)S(1)} %get-tuple-element.36), channel_id=1, source_target_pairs={{0,2},{4,6},{8,10},{12,14},{16,18},{20,22},{24,26},{28,30},{32,34}... | collective-permute-start | bytes 147464 | tf_op jit(solution)/shard_map/ppermute | solution.py:404
  36.5 10.6 %collective-permute-start.6 = (f32[96,128]{1,0:T(8,128)S(1)}, f32[96,128]{1,0:T(8,128)S(1)}, u32[]{:S(2)}, u32[]{:S(2)}) collective-permute-start(f32[96,128]{1,0:T(8,128)S(1)} %get-tuple-element.39), channel_id=1, source_target_pairs={{64,128},{192,256},{320,384},{448,512},{576,640},{128,64},{256,192... | collective-permute-start | bytes 147464 | tf_op jit(solution)/shard_map/ppermute | solution.py:404
  38.4 8.7 %collective-permute-start.7 = (f32[96,128]{1,0:T(8,128)S(1)}, f32[96,128]{1,0:T(8,128)S(1)}, u32[]{:S(2)}, u32[]{:S(2)}) collective-permute-start(f32[96,128]{1,0:T(8,128)S(1)} %get-tuple-element.40), channel_id=1, source_target_pairs={{0,64},{128,192},{256,320},{384,448},{512,576},{640,704},{64,0},{1... | collective-permute-start | bytes 147464 | tf_op jit(solution)/shard_map/ppermute | solution.py:404

commit v4 on v3

--- a/solution.py
+++ b/solution.py
@@ -51,6 +51,13 @@
 
 def iota(shape, dim):
     return lax.broadcasted_iota(jnp.int32, shape, dim)
+
+
+def spread(mixing, lanes):
+    return [
+        [jnp.broadcast_to(mixing[pl.ds(v, 1), pl.ds(w, 1)], (ROWS, lanes)) for w in range(VARS)]
+        for v in range(VARS)
+    ]
 
 
 def moved_mask(agg_ref, plane):
@@ -164,7 +171,7 @@
 def inner_kernel(mixing, state, forcing, coef, partial):
     lane = iota((ROWS, NZ), 1)
     row = iota((ROWS, NZ), 0)
-    mix = [[mixing[v, w] for w in range(VARS)] for v in range(VARS)]
+    mix = spread(mixing, NZ)
     for x in range(PLANES):
         c = coef[pl.ds(x * ROWS, ROWS), :]
         for i in range(HERE):
@@ -283,7 +290,7 @@
 
 def second_kernel(mixing, r_win, s_win, delta, partial):
     lane = iota((ROWS, CZ), 1)
-    mix = [[mixing[v, w] for w in range(VARS)] for v in range(VARS)]
+    mix = spread(mixing, CZ)
     for p in range(2):
         inverse, coef_c, scale = damping(s_win[window(p, FIELDS), :], r_win[window(p, FIELDS), :])
         for i in range(HERE):
@@ -362,7 +369,6 @@
 
 
 VMEM = pl.BlockSpec(memory_space=pltpu.VMEM)
-SMEM = pl.BlockSpec(memory_space=pltpu.SMEM)
 HBM = pl.BlockSpec(memory_space=pltpu.HBM)
 
 
@@ -407,7 +413,7 @@
     sums = (WIN * ROWS, NZ)
     rims = (2, WIN * ROWS, 128)
     x_face = (FIELDS * ROWS, NZ)
-    y_face = (120, NZ)
+    y_face = (64 + WIN, NZ)
     yb, xb, xa, ya, state, forcing, coef, agg, s_win = call(
         edges_kernel,
         [y_face, x_face, x_face, y_face, fine, fine, coef.shape, agg, wins],
@@ -421,7 +427,7 @@
     xa = swap(xa, "sx")
     ya = swap(ya, "sy")
     other = lax.all_gather(state, "hb")
-    (partial,) = call(inner_kernel, [fine], [], mixing, state, forcing, coef, spaces=[SMEM])
+    (partial,) = call(inner_kernel, [fine], [], mixing, state, forcing, coef)
     msg = (3 * WIN, CZ)
     mb, ma, residual, r_win, s_win = call(
         outer_kernel,
@@ -441,7 +447,7 @@
     db = swap(db, "sx", 1)
     da = swap(da, "sx")
     other_delta = lax.all_gather(delta, "hb")
-    (step,) = call(second_kernel, [wins], [], mixing, r_win, s_win, delta, spaces=[SMEM])
+    (step,) = call(second_kernel, [wins], [], mixing, r_win, s_win, delta)
     (corrected,) = call(
         final_kernel,
         [fine],

time: 48.6 us -> 47.1 us (0.969)
  the two profiles are of different devices: /device:TPU:253 before, /device:TPU:254 now
where the time goes in v4:
time: 47.1 us; the launch traced here: 46.8 us
  starting transfers between devices  29.4 us (62%)
  waiting for transfers between devices  7.34 us (16%)
  Pallas kernels  4.79 us (10%)
  blocking collectives  4.5 us (10%)
  between operations  0.76 us (2%)
    ppermute x8, starting transfers between devices, swap(): return lax.ppermute(value, axis, swap_pairs(axis, first))  29.4 us
    ppermute x8, waiting for transfers between devices, swap(): return lax.ppermute(value, axis, swap_pairs(axis, first))  7.34 us
    pallas_call x7, Pallas kernels, call(): pl.pallas_call(kernel, out_shape=outs, in_specs=spaces, out_specs=out_spa...  4.79 us
    all_gather x1, blocking collectives, shards(): other = lax.all_gather(state, 'hb')  2.51 us
    all_gather x1, blocking collectives, shards(): other_delta = lax.all_gather(delta, 'hb')  1.99 us
  transfers between devices with their start and end apart: 8, of which 5 were waited for; matrix products, arithmetic and copies ran while one was open for 0% of the time, Pallas kernels for 4%

profile of v4, /device:TPU:254, one launch (start us, length us, event | category | flops | bytes accessed | tf_op | source)
XLA Modules:
  0.0 46.8 jit_solution(6080110509423428768)
XLA Ops:
  0.6 1.4 %edges_kernel.1 = (f32[96,256]{1,0:T(8,128)S(1)}, f32[120,256]{1,0:T(8,128)S(1)}, f32[120,256]{1,0:T(8,128)S(1)}, f32[96,256]{1,0:T(8,128)S(1)}, f32[480,256]{1,...) custom-call(f32[480,256]{1,0:T(8,128)} %bitcast.10, ...), custom_call_target="tpu_custom_call" | custom-call | tf_op jit(solution)/shard_map/edges_kernel/pallas_call | solution.py:382
  2.0 8.3 %collective-permute-start = (f32[96,256]{1,0:T(8,128)S(1)}, f32[96,256]{1,0:T(8,128)S(1)}, u32[]{:S(2)}, u32[]{:S(2)}) collective-permute-start(f32[96,256]{1,0:T(8,128)S(1)} %get-tuple-element.25), channel_id=1, source_target_pairs={{2,4},{6,8},{10,12},{14,16},{18,20},{22,24},{26,28},{30,32},{34,36... | collective-permute-start | bytes 294920 | tf_op jit(solution)/shard_map/ppermute | solution.py:410
  10.3 1.9 %collective-permute-start.1 = (f32[96,256]{1,0:T(8,128)S(1)}, f32[96,256]{1,0:T(8,128)S(1)}, u32[]{:S(2)}, u32[]{:S(2)}) collective-permute-start(f32[96,256]{1,0:T(8,128)S(1)} %get-tuple-element.26), channel_id=1, source_target_pairs={{0,2},{4,6},{8,10},{12,14},{16,18},{20,22},{24,26},{28,30},{32,34}... | collective-permute-start | bytes 294920 | tf_op jit(solution)/shard_map/ppermute | solution.py:410
  12.3 3.9 %collective-permute-start.2 = (f32[120,256]{1,0:T(8,128)S(1)}, f32[120,256]{1,0:T(8,128)S(1)}, u32[]{:S(2)}, u32[]{:S(2)}) collective-permute-start(f32[120,256]{1,0:T(8,128)S(1)} %get-tuple-element.27), channel_id=1, source_target_pairs={{64,128},{192,256},{320,384},{448,512},{576,640},{128,64},{256,192... | collective-permute-start | bytes 368648 | tf_op jit(solution)/shard_map/ppermute | solution.py:410
  16.2 1.9 %collective-permute-start.3 = (f32[120,256]{1,0:T(8,128)S(1)}, f32[120,256]{1,0:T(8,128)S(1)}, u32[]{:S(2)}, u32[]{:S(2)}) collective-permute-start(f32[120,256]{1,0:T(8,128)S(1)} %get-tuple-element.28), channel_id=1, source_target_pairs={{0,64},{128,192},{256,320},{384,448},{512,576},{640,704},{64,0},{1... | collective-permute-start | bytes 368648 | tf_op jit(solution)/shard_map/ppermute | solution.py:410
  18.1 0.0 copy-start
  18.1 2.5 %all-gather = f32[960,256]{1,0:T(8,128)S(1)} all-gather(f32[480,256]{1,0:T(8,128)S(1)} %get-tuple-element.22.state), channel_id=2, replica_groups=mesh['sx'=12,'sy'=32,'hb'=2] {'hb'}, dimensions={0}, use_global_device_ids=true | all-gather | bytes 1474560 | tf_op jit(solution)/shard_map/all_gather | solution.py:429
  20.6 0.0 copy-done
  20.6 0.6 %inner_kernel.1.partial = f32[480,256]{1,0:T(8,128)S(1)} custom-call(f32[5,5]{1,0:T(8,128)S(1)} %copy-done, f32[480,256]{1,0:T(8,128)S(1)} %get-tuple-element.22.state, f32[480,256]{1,0:T(8,128)S(1)} %get-tuple-element.23.forcing, f32[32,256]{1,0:T(8,128)S(1)} %get-tuple-element.24.coef), custom_call_target="tpu_custom_call" | custom-call | tf_op jit(solution)/shard_map/inner_kernel/pallas_call | solution.py:382
  21.2 0.0 collective-permute-done.yb
  21.3 0.0 collective-permute-done.1.ya
  21.3 1.1 %collective-permute-done.2.xb = f32[120,256]{1,0:T(8,128)S(1)} collective-permute-done((f32[120,256]{1,0:T(8,128)S(1)}, f32[120,256]{1,0:T(8,128)S(1)}, u32[]{:S(2)}, u32[]{:S(2)}) %collective-permute-start.2) | collective-permute-done | bytes 122912 | tf_op jit(solution)/shard_map/ppermute | solution.py:410
  22.4 0.6 %collective-permute-done.3.xa = f32[120,256]{1,0:T(8,128)S(1)} collective-permute-done((f32[120,256]{1,0:T(8,128)S(1)}, f32[120,256]{1,0:T(8,128)S(1)}, u32[]{:S(2)}, u32[]{:S(2)}) %collective-permute-start.3) | collective-permute-done | bytes 122912 | tf_op jit(solution)/shard_map/ppermute | solution.py:410
  23.0 0.5 %outer_kernel.1 = (f32[96,128]{1,0:T(8,128)S(1)}, f32[96,128]{1,0:T(8,128)S(1)}, f32[480,256]{1,0:T(8,128)S(1)}, f32[256,128]{1,0:T(8,128)S(1)}, f32[256,128]{1,0:T(8,128)S(1)}) custom-call(f32[480,256]{1,0:T(8,128)S(1)} %inner_kernel.1.partial, f32[96,256]{1,0:T(8,128)S(1)} %collective-permute-done.yb, f32[96,256]{1,0:T(8,128)S(1)} %collective-permute-done.1.ya, ...), custom_call_target="tpu_custom_call" | custom-call | tf_op jit(solution)/shard_map/outer_kernel/pallas_call | solution.py:382
  23.5 5.0 %collective-permute-start.4 = (f32[96,128]{1,0:T(8,128)S(1)}, f32[96,128]{1,0:T(8,128)S(1)}, u32[]{:S(2)}, u32[]{:S(2)}) collective-permute-start(f32[96,128]{1,0:T(8,128)S(1)} %get-tuple-element.35), channel_id=1, source_target_pairs={{2,4},{6,8},{10,12},{14,16},{18,20},{22,24},{26,28},{30,32},{34,36... | collective-permute-start | bytes 147464 | tf_op jit(solution)/shard_map/ppermute | solution.py:410
  28.5 1.9 %collective-permute-start.5 = (f32[96,128]{1,0:T(8,128)S(1)}, f32[96,128]{1,0:T(8,128)S(1)}, u32[]{:S(2)}, u32[]{:S(2)}) collective-permute-start(f32[96,128]{1,0:T(8,128)S(1)} %get-tuple-element.36), channel_id=1, source_target_pairs={{0,2},{4,6},{8,10},{12,14},{16,18},{20,22},{24,26},{28,30},{32,34}... | collective-permute-start | bytes 147464 | tf_op jit(solution)/shard_map/ppermute | solution.py:410
  30.5 0.8 %store_kernel.1 = (f32[480,256]{1,0:T(8,128)}, f32[256,128]{1,0:T(8,128)S(1)}) custom-call(f32[480,256]{1,0:T(8,128)S(1)} %get-tuple-element.31.values, f32[256,128]{1,0:T(8,128)S(1)} %get-tuple-element.32.r_in), custom_call_target="tpu_custom_call" | custom-call | tf_op jit(solution)/shard_map/store_kernel/pallas_call | solution.py:382
  31.3 3.8 %collective-permute-done.4.mb = f32[96,128]{1,0:T(8,128)S(1)} collective-permute-done((f32[96,128]{1,0:T(8,128)S(1)}, f32[96,128]{1,0:T(8,128)S(1)}, u32[]{:S(2)}, u32[]{:S(2)}) %collective-permute-start.4) | collective-permute-done | bytes 49184 | tf_op jit(solution)/shard_map/ppermute | solution.py:410
  35.1 0.0 collective-permute-done.5.ma
  35.1 0.1 first_kernel.1
  35.2 4.4 %collective-permute-start.6 = (f32[96,128]{1,0:T(8,128)S(1)}, f32[96,128]{1,0:T(8,128)S(1)}, u32[]{:S(2)}, u32[]{:S(2)}) collective-permute-start(f32[96,128]{1,0:T(8,128)S(1)} %get-tuple-element.39), channel_id=1, source_target_pairs={{64,128},{192,256},{320,384},{448,512},{576,640},{128,64},{256,192... | collective-permute-start | bytes 147464 | tf_op jit(solution)/shard_map/ppermute | solution.py:410
  39.6 1.9 %collective-permute-start.7 = (f32[96,128]{1,0:T(8,128)S(1)}, f32[96,128]{1,0:T(8,128)S(1)}, u32[]{:S(2)}, u32[]{:S(2)}) collective-permute-start(f32[96,128]{1,0:T(8,128)S(1)} %get-tuple-element.40), channel_id=1, source_target_pairs={{0,64},{128,192},{256,320},{384,448},{512,576},{640,704},{64,0},{1... | collective-permute-start | bytes 147464 | tf_op jit(solution)/shard_map/ppermute | solution.py:410
  41.6 0.3 second_kernel.1.partial
  41.8 2.0 %all-gather.1 = f32[512,128]{1,0:T(8,128)S(1)} all-gather(f32[256,128]{1,0:T(8,128)S(1)} %get-tuple-element.38.delta), channel_id=3, replica_groups=mesh['sx'=12,'sy'=32,'hb'=2] {'hb'}, dimensions={0}, use_global_device_ids=true | all-gather | bytes 393216 | tf_op jit(solution)/shard_map/all_gather | solution.py:449
  43.8 0.7 %collective-permute-done.6.xb = f32[96,128]{1,0:T(8,128)S(1)} collective-permute-done((f32[96,128]{1,0:T(8,128)S(1)}, f32[96,128]{1,0:T(8,128)S(1)}, u32[]{:S(2)}, u32[]{:S(2)}) %collective-permute-start.6) | collective-permute-done | bytes 49184 | tf_op jit(solution)/shard_map/ppermute | solution.py:410
  44.5 1.1 %collective-permute-done.7.xa = f32[96,128]{1,0:T(8,128)S(1)} collective-permute-done((f32[96,128]{1,0:T(8,128)S(1)}, f32[96,128]{1,0:T(8,128)S(1)}, u32[]{:S(2)}, u32[]{:S(2)}) %collective-permute-start.7) | collective-permute-done | bytes 49184 | tf_op jit(solution)/shard_map/ppermute | solution.py:410
  45.6 1.1 %final_kernel.1 = f32[480,256]{1,0:T(8,128)} custom-call(f32[256,128]{1,0:T(8,128)S(1)} %second_kernel.1.partial, f32[96,128]{1,0:T(8,128)S(1)} %collective-permute-done.6.xb, f32[96,128]{1,0:T(8,128)S(1)} %collective-permute-done.7.xa, f32[2,256,128]{2,1,0:T(8,128)S(1)} %bitcast.9, f32[480,256]{1,0:T(8,128)S(1)} %get-tuple-element.22.state, ...), custom_call_target="tpu_custom_call" | custom-call | tf_op jit(solution)/shard_map/final_kernel/pallas_call | solution.py:382
Async XLA Ops:
  2.0 19.2 %collective-permute-start = (f32[96,256]{1,0:T(8,128)S(1)}, f32[96,256]{1,0:T(8,128)S(1)}, u32[]{:S(2)}, u32[]{:S(2)}) collective-permute-start(f32[96,256]{1,0:T(8,128)S(1)} %get-tuple-element.25), channel_id=1, source_target_pairs={{2,4},{6,8},{10,12},{14,16},{18,20},{22,24},{26,28},{30,32},{34,36... | collective-permute-start | bytes 294920 | tf_op jit(solution)/shard_map/ppermute | solution.py:410
  10.3 10.9 %collective-permute-start.1 = (f32[96,256]{1,0:T(8,128)S(1)}, f32[96,256]{1,0:T(8,128)S(1)}, u32[]{:S(2)}, u32[]{:S(2)}) collective-permute-start(f32[96,256]{1,0:T(8,128)S(1)} %get-tuple-element.26), channel_id=1, source_target_pairs={{0,2},{4,6},{8,10},{12,14},{16,18},{20,22},{24,26},{28,30},{32,34}... | collective-permute-start | bytes 294920 | tf_op jit(solution)/shard_map/ppermute | solution.py:410
  12.3 10.1 %collective-permute-start.2 = (f32[120,256]{1,0:T(8,128)S(1)}, f32[120,256]{1,0:T(8,128)S(1)}, u32[]{:S(2)}, u32[]{:S(2)}) collective-permute-start(f32[120,256]{1,0:T(8,128)S(1)} %get-tuple-element.27), channel_id=1, source_target_pairs={{64,128},{192,256},{320,384},{448,512},{576,640},{128,64},{256,192... | collective-permute-start | bytes 368648 | tf_op jit(solution)/shard_map/ppermute | solution.py:410
  16.2 6.8 %collective-permute-start.3 = (f32[120,256]{1,0:T(8,128)S(1)}, f32[120,256]{1,0:T(8,128)S(1)}, u32[]{:S(2)}, u32[]{:S(2)}) collective-permute-start(f32[120,256]{1,0:T(8,128)S(1)} %get-tuple-element.28), channel_id=1, source_target_pairs={{0,64},{128,192},{256,320},{384,448},{512,576},{640,704},{64,0},{1... | collective-permute-start | bytes 368648 | tf_op jit(solution)/shard_map/ppermute | solution.py:410
  18.1 2.5 %copy-start = (f32[5,5]{1,0:T(8,128)S(1)}, f32[5,5]{1,0:T(8,128)}, u32[]{:S(2)}) copy-start(f32[5,5]{1,0:T(8,128)} %mixing.3) | copy-start | bytes 304
  23.5 11.6 %collective-permute-start.4 = (f32[96,128]{1,0:T(8,128)S(1)}, f32[96,128]{1,0:T(8,128)S(1)}, u32[]{:S(2)}, u32[]{:S(2)}) collective-permute-start(f32[96,128]{1,0:T(8,128)S(1)} %get-tuple-element.35), channel_id=1, source_target_pairs={{2,4},{6,8},{10,12},{14,16},{18,20},{22,24},{26,28},{30,32},{34,36... | collective-permute-start | bytes 147464 | tf_op jit(solution)/shard_map/ppermute | solution.py:410
  28.5 6.6 %collective-permute-start.5 = (f32[96,128]{1,0:T(8,128)S(1)}, f32[96,128]{1,0:T(8,128)S(1)}, u32[]{:S(2)}, u32[]{:S(2)}) collective-permute-start(f32[96,128]{1,0:T(8,128)S(1)} %get-tuple-element.36), channel_id=1, source_target_pairs={{0,2},{4,6},{8,10},{12,14},{16,18},{20,22},{24,26},{28,30},{32,34}... | collective-permute-start | bytes 147464 | tf_op jit(solution)/shard_map/ppermute | solution.py:410
  35.2 9.3 %collective-permute-start.6 = (f32[96,128]{1,0:T(8,128)S(1)}, f32[96,128]{1,0:T(8,128)S(1)}, u32[]{:S(2)}, u32[]{:S(2)}) collective-permute-start(f32[96,128]{1,0:T(8,128)S(1)} %get-tuple-element.39), channel_id=1, source_target_pairs={{64,128},{192,256},{320,384},{448,512},{576,640},{128,64},{256,192... | collective-permute-start | bytes 147464 | tf_op jit(solution)/shard_map/ppermute | solution.py:410
  39.6 6.0 %collective-permute-start.7 = (f32[96,128]{1,0:T(8,128)S(1)}, f32[96,128]{1,0:T(8,128)S(1)}, u32[]{:S(2)}, u32[]{:S(2)}) collective-permute-start(f32[96,128]{1,0:T(8,128)S(1)} %get-tuple-element.40), channel_id=1, source_target_pairs={{0,64},{128,192},{256,320},{384,448},{512,576},{640,704},{64,0},{1... | collective-permute-start | bytes 147464 | tf_op jit(solution)/shard_map/ppermute | solution.py:410

commit v5 on v4

--- a/solution.py
+++ b/solution.py
@@ -202,27 +202,17 @@
     return inverse, coef_c, 0.6 / (6.0 * coef_c + 2.0)
 
 
-def outer_kernel(
-    partial, yb, ya, xb, xa, other, coef, agg, s_in,
-    mb, ma, residual, r_win, s_win, sums, rims, summed, edge, scaled, halves, coefs,
-):
-    even_x, even_y = (even_index("sx"), even_index("sy"))
+def rows_kernel(partial, yb, ya, other, coef, s_in, halves, s_win, edge, coefs):
+    even_y = even_index("sy")
     peer = 1 - lax.axis_index("hb")
     for x in range(PLANES):
-        c = coef[pl.ds(x * ROWS, ROWS), :]
         for i in range(HERE):
             for v in range(VARS):
-                field = i * VARS + v
-                face = pl.ds(field * ROWS, ROWS)
-                total = partial[tile(field, x), :]
+                total = partial[tile(i * VARS + v, x), :]
                 for j in range(HERE):
                     total = total - OTHER[i][j] * other[peer, tile(j * VARS + v, x), :]
-                if x == 0:
-                    total = total + c * choose(even_x, xb[face, :], xa[face, :])
-                if x == PLANES - 1:
-                    total = total + c * choose(even_x, xa[face, :], xb[face, :])
                 for half in range(2):
-                    halves[half, tile(field, x), :] = total[:, half * 128 : (half + 1) * 128]
+                    halves[half, tile(i * VARS + v, x), :] = total[:, half * 128 : (half + 1) * 128]
     count = FIELDS * PLANES
     for half in range(2):
         lanes = pl.ds(half * 128, 128)
@@ -236,14 +226,29 @@
             c60 = jnp.concatenate([c8] * (count // 8) + [c8[: count % 8]], axis=0)
             rows = pl.ds(y, count, stride=ROWS)
             halves[half, rows, :] = halves[half, rows, :] + c60 * halo
-        residual[:, lanes] = halves[half]
-    restrict(residual, lambda x: jnp.ones((ROWS, NZ), F32), agg, r_win, sums, rims, summed)
     s_win[...] = s_in[...]
     for half, (above, below) in enumerate(((6, 1), (5, 2))):
         lanes = pl.ds(half * 128, 128)
         at_a, at_b = (ya[pl.ds(64, WIN), lanes], yb[pl.ds(64, WIN), lanes])
         s_win[row_of(below), :] = s_win[row_of(below), :] + choose(even_y, at_b, at_a)
         s_win[row_of(above), :] = s_win[row_of(above), :] + choose(even_y, at_a, at_b)
+
+
+def outer_kernel(
+    partial, xb, xa, coef, agg, s_win, mb, ma, residual, r_win, sums, rims, summed, scaled
+):
+    even_x, even_y = (even_index("sx"), even_index("sy"))
+    for x in range(PLANES):
+        c = coef[pl.ds(x * ROWS, ROWS), :]
+        for field in range(FIELDS):
+            face = pl.ds(field * ROWS, ROWS)
+            total = jnp.concatenate([partial[h, tile(field, x), :] for h in range(2)], axis=1)
+            if x == 0:
+                total = total + c * choose(even_x, xb[face, :], xa[face, :])
+            if x == PLANES - 1:
+                total = total + c * choose(even_x, xa[face, :], xb[face, :])
+            residual[tile(field, x), :] = total
+    restrict(residual, lambda x: jnp.ones((ROWS, NZ), F32), agg, r_win, sums, rims, summed)
     for p in range(2):
         _, _, scale = damping(s_win[window(p, FIELDS), :], r_win[window(p, FIELDS), :])
         for field in range(GROUP):
@@ -429,11 +434,17 @@
     other = lax.all_gather(state, "hb")
     (partial,) = call(inner_kernel, [fine], [], mixing, state, forcing, coef)
     msg = (3 * WIN, CZ)
-    mb, ma, residual, r_win, s_win = call(
+    partial, s_win = call(
+        rows_kernel,
+        [halves, wins],
+        [(8, 128), (2, PLANES * ROWS, 128)],
+        partial, yb, ya, other, coef, s_win,
+    )
+    mb, ma, residual, r_win = call(
         outer_kernel,
-        [msg, msg, fine, wins, wins],
-        [sums, rims, wins, (8, 128), wins, halves, (2, PLANES * ROWS, 128)],
-        partial, yb, ya, xb, xa, other, coef, agg, s_win,
+        [msg, msg, fine, wins],
+        [sums, rims, wins, wins],
+        partial, xb, xa, coef, agg, s_win,
     )
     mb = swap(mb, "sy", 1)
     ma = swap(ma, "sy")

time: 47.1 us -> 46.6 us (0.989)
  the two profiles are of different devices: /device:TPU:254 before, /device:TPU:250 now
where the time goes in v5:
time: 46.6 us; the launch traced here: 46.3 us
  starting transfers between devices  29 us (62%)
  waiting for transfers between devices  7.14 us (15%)
  Pallas kernels  4.82 us (10%)
  blocking collectives  4.5 us (10%)
  between operations  0.78 us (2%)
    ppermute x8, starting transfers between devices, swap(): return lax.ppermute(value, axis, swap_pairs(axis, first))  29 us
    ppermute x8, waiting for transfers between devices, swap(): return lax.ppermute(value, axis, swap_pairs(axis, first))  7.14 us
    pallas_call x8, Pallas kernels, call(): pl.pallas_call(kernel, out_shape=outs, in_specs=spaces, out_specs=out_spa...  4.82 us
    all_gather x1, blocking collectives, shards(): other = lax.all_gather(state, 'hb')  2.51 us
    all_gather x1, blocking collectives, shards(): other_delta = lax.all_gather(delta, 'hb')  1.99 us
  transfers between devices with their start and end apart: 8, of which 3 were waited for; matrix products, arithmetic and copies ran while one was open for 0% of the time, Pallas kernels for 4%

profile of v5, /device:TPU:250, one launch (start us, length us, event | category | flops | bytes accessed | tf_op | source)
XLA Modules:
  0.0 46.3 jit_solution(555575155866735396)
XLA Ops:
  0.6 1.4 %edges_kernel.1 = (f32[96,256]{1,0:T(8,128)S(1)}, f32[120,256]{1,0:T(8,128)S(1)}, f32[120,256]{1,0:T(8,128)S(1)}, f32[96,256]{1,0:T(8,128)S(1)}, f32[480,256]{1,...) custom-call(f32[480,256]{1,0:T(8,128)} %bitcast.10, ...), custom_call_target="tpu_custom_call" | custom-call | tf_op jit(solution)/shard_map/edges_kernel/pallas_call | solution.py:387
  2.0 8.3 %collective-permute-start = (f32[96,256]{1,0:T(8,128)S(1)}, f32[96,256]{1,0:T(8,128)S(1)}, u32[]{:S(2)}, u32[]{:S(2)}) collective-permute-start(f32[96,256]{1,0:T(8,128)S(1)} %get-tuple-element.26), channel_id=1, source_target_pairs={{2,4},{6,8},{10,12},{14,16},{18,20},{22,24},{26,28},{30,32},{34,36... | collective-permute-start | bytes 294920 | tf_op jit(solution)/shard_map/ppermute | solution.py:415
  10.3 1.9 %collective-permute-start.1 = (f32[96,256]{1,0:T(8,128)S(1)}, f32[96,256]{1,0:T(8,128)S(1)}, u32[]{:S(2)}, u32[]{:S(2)}) collective-permute-start(f32[96,256]{1,0:T(8,128)S(1)} %get-tuple-element.27), channel_id=1, source_target_pairs={{0,2},{4,6},{8,10},{12,14},{16,18},{20,22},{24,26},{28,30},{32,34}... | collective-permute-start | bytes 294920 | tf_op jit(solution)/shard_map/ppermute | solution.py:415
  12.3 3.4 %collective-permute-start.2 = (f32[120,256]{1,0:T(8,128)S(1)}, f32[120,256]{1,0:T(8,128)S(1)}, u32[]{:S(2)}, u32[]{:S(2)}) collective-permute-start(f32[120,256]{1,0:T(8,128)S(1)} %get-tuple-element.30), channel_id=1, source_target_pairs={{64,128},{192,256},{320,384},{448,512},{576,640},{128,64},{256,192... | collective-permute-start | bytes 368648 | tf_op jit(solution)/shard_map/ppermute | solution.py:415
  15.7 1.9 %collective-permute-start.3 = (f32[120,256]{1,0:T(8,128)S(1)}, f32[120,256]{1,0:T(8,128)S(1)}, u32[]{:S(2)}, u32[]{:S(2)}) collective-permute-start(f32[120,256]{1,0:T(8,128)S(1)} %get-tuple-element.31), channel_id=1, source_target_pairs={{0,64},{128,192},{256,320},{384,448},{512,576},{640,704},{64,0},{1... | collective-permute-start | bytes 368648 | tf_op jit(solution)/shard_map/ppermute | solution.py:415
  17.6 0.0 copy-start
  17.6 2.5 %all-gather = f32[960,256]{1,0:T(8,128)S(1)} all-gather(f32[480,256]{1,0:T(8,128)S(1)} %get-tuple-element.23.state), channel_id=2, replica_groups=mesh['sx'=12,'sy'=32,'hb'=2] {'hb'}, dimensions={0}, use_global_device_ids=true | all-gather | bytes 1474560 | tf_op jit(solution)/shard_map/all_gather | solution.py:434
  20.1 0.0 copy-done
  20.1 0.6 %inner_kernel.1.partial = f32[480,256]{1,0:T(8,128)S(1)} custom-call(f32[5,5]{1,0:T(8,128)S(1)} %copy-done, f32[480,256]{1,0:T(8,128)S(1)} %get-tuple-element.23.state, f32[480,256]{1,0:T(8,128)S(1)} %get-tuple-element.24.forcing, f32[32,256]{1,0:T(8,128)S(1)} %get-tuple-element.25.coef), custom_call_target="tpu_custom_call" | custom-call | tf_op jit(solution)/shard_map/inner_kernel/pallas_call | solution.py:387
  20.7 0.0 collective-permute-done.yb
  20.8 0.0 collective-permute-done.1.ya
  20.8 0.2 rows_kernel.1
  21.0 0.0 collective-permute-done.2.xb
  21.0 1.5 %collective-permute-done.3.xa = f32[120,256]{1,0:T(8,128)S(1)} collective-permute-done((f32[120,256]{1,0:T(8,128)S(1)}, f32[120,256]{1,0:T(8,128)S(1)}, u32[]{:S(2)}, u32[]{:S(2)}) %collective-permute-start.3) | collective-permute-done | bytes 122912 | tf_op jit(solution)/shard_map/ppermute | solution.py:415
  22.5 0.4 outer_kernel.1
  22.8 5.0 %collective-permute-start.4 = (f32[96,128]{1,0:T(8,128)S(1)}, f32[96,128]{1,0:T(8,128)S(1)}, u32[]{:S(2)}, u32[]{:S(2)}) collective-permute-start(f32[96,128]{1,0:T(8,128)S(1)} %get-tuple-element.37), channel_id=1, source_target_pairs={{2,4},{6,8},{10,12},{14,16},{18,20},{22,24},{26,28},{30,32},{34,36... | collective-permute-start | bytes 147464 | tf_op jit(solution)/shard_map/ppermute | solution.py:415
  27.9 1.9 %collective-permute-start.5 = (f32[96,128]{1,0:T(8,128)S(1)}, f32[96,128]{1,0:T(8,128)S(1)}, u32[]{:S(2)}, u32[]{:S(2)}) collective-permute-start(f32[96,128]{1,0:T(8,128)S(1)} %get-tuple-element.38), channel_id=1, source_target_pairs={{0,2},{4,6},{8,10},{12,14},{16,18},{20,22},{24,26},{28,30},{32,34}... | collective-permute-start | bytes 147464 | tf_op jit(solution)/shard_map/ppermute | solution.py:415
  29.8 0.8 %store_kernel.1 = (f32[480,256]{1,0:T(8,128)}, f32[256,128]{1,0:T(8,128)S(1)}) custom-call(f32[480,256]{1,0:T(8,128)S(1)} %get-tuple-element.34.values, f32[256,128]{1,0:T(8,128)S(1)} %get-tuple-element.35.r_in), custom_call_target="tpu_custom_call" | custom-call | tf_op jit(solution)/shard_map/store_kernel/pallas_call | solution.py:387
  30.6 3.8 %collective-permute-done.4.mb = f32[96,128]{1,0:T(8,128)S(1)} collective-permute-done((f32[96,128]{1,0:T(8,128)S(1)}, f32[96,128]{1,0:T(8,128)S(1)}, u32[]{:S(2)}, u32[]{:S(2)}) %collective-permute-start.4) | collective-permute-done | bytes 49184 | tf_op jit(solution)/shard_map/ppermute | solution.py:415
  34.4 0.0 collective-permute-done.5.ma
  34.5 0.1 first_kernel.1
  34.5 4.6 %collective-permute-start.6 = (f32[96,128]{1,0:T(8,128)S(1)}, f32[96,128]{1,0:T(8,128)S(1)}, u32[]{:S(2)}, u32[]{:S(2)}) collective-permute-start(f32[96,128]{1,0:T(8,128)S(1)} %get-tuple-element.41), channel_id=1, source_target_pairs={{64,128},{192,256},{320,384},{448,512},{576,640},{128,64},{256,192... | collective-permute-start | bytes 147464 | tf_op jit(solution)/shard_map/ppermute | solution.py:415
  39.1 1.9 %collective-permute-start.7 = (f32[96,128]{1,0:T(8,128)S(1)}, f32[96,128]{1,0:T(8,128)S(1)}, u32[]{:S(2)}, u32[]{:S(2)}) collective-permute-start(f32[96,128]{1,0:T(8,128)S(1)} %get-tuple-element.42), channel_id=1, source_target_pairs={{0,64},{128,192},{256,320},{384,448},{512,576},{640,704},{64,0},{1... | collective-permute-start | bytes 147464 | tf_op jit(solution)/shard_map/ppermute | solution.py:415
  41.1 0.3 second_kernel.1.partial
  41.3 2.0 %all-gather.1 = f32[512,128]{1,0:T(8,128)S(1)} all-gather(f32[256,128]{1,0:T(8,128)S(1)} %get-tuple-element.40.delta), channel_id=3, replica_groups=mesh['sx'=12,'sy'=32,'hb'=2] {'hb'}, dimensions={0}, use_global_device_ids=true | all-gather | bytes 393216 | tf_op jit(solution)/shard_map/all_gather | solution.py:460
  43.3 0.0 collective-permute-done.6.xb
  43.3 1.8 %collective-permute-done.7.xa = f32[96,128]{1,0:T(8,128)S(1)} collective-permute-done((f32[96,128]{1,0:T(8,128)S(1)}, f32[96,128]{1,0:T(8,128)S(1)}, u32[]{:S(2)}, u32[]{:S(2)}) %collective-permute-start.7) | collective-permute-done | bytes 49184 | tf_op jit(solution)/shard_map/ppermute | solution.py:415
  45.1 1.1 %final_kernel.1 = f32[480,256]{1,0:T(8,128)} custom-call(f32[256,128]{1,0:T(8,128)S(1)} %second_kernel.1.partial, f32[96,128]{1,0:T(8,128)S(1)} %collective-permute-done.6.xb, f32[96,128]{1,0:T(8,128)S(1)} %collective-permute-done.7.xa, f32[2,256,128]{2,1,0:T(8,128)S(1)} %bitcast.9, f32[480,256]{1,0:T(8,128)S(1)} %get-tuple-element.23.state, ...), custom_call_target="tpu_custom_call" | custom-call | tf_op jit(solution)/shard_map/final_kernel/pallas_call | solution.py:387
Async XLA Ops:
  2.0 18.7 %collective-permute-start = (f32[96,256]{1,0:T(8,128)S(1)}, f32[96,256]{1,0:T(8,128)S(1)}, u32[]{:S(2)}, u32[]{:S(2)}) collective-permute-start(f32[96,256]{1,0:T(8,128)S(1)} %get-tuple-element.26), channel_id=1, source_target_pairs={{2,4},{6,8},{10,12},{14,16},{18,20},{22,24},{26,28},{30,32},{34,36... | collective-permute-start | bytes 294920 | tf_op jit(solution)/shard_map/ppermute | solution.py:415
  10.3 10.4 %collective-permute-start.1 = (f32[96,256]{1,0:T(8,128)S(1)}, f32[96,256]{1,0:T(8,128)S(1)}, u32[]{:S(2)}, u32[]{:S(2)}) collective-permute-start(f32[96,256]{1,0:T(8,128)S(1)} %get-tuple-element.27), channel_id=1, source_target_pairs={{0,2},{4,6},{8,10},{12,14},{16,18},{20,22},{24,26},{28,30},{32,34}... | collective-permute-start | bytes 294920 | tf_op jit(solution)/shard_map/ppermute | solution.py:415
  12.3 8.7 %collective-permute-start.2 = (f32[120,256]{1,0:T(8,128)S(1)}, f32[120,256]{1,0:T(8,128)S(1)}, u32[]{:S(2)}, u32[]{:S(2)}) collective-permute-start(f32[120,256]{1,0:T(8,128)S(1)} %get-tuple-element.30), channel_id=1, source_target_pairs={{64,128},{192,256},{320,384},{448,512},{576,640},{128,64},{256,192... | collective-permute-start | bytes 368648 | tf_op jit(solution)/shard_map/ppermute | solution.py:415
  15.7 6.8 %collective-permute-start.3 = (f32[120,256]{1,0:T(8,128)S(1)}, f32[120,256]{1,0:T(8,128)S(1)}, u32[]{:S(2)}, u32[]{:S(2)}) collective-permute-start(f32[120,256]{1,0:T(8,128)S(1)} %get-tuple-element.31), channel_id=1, source_target_pairs={{0,64},{128,192},{256,320},{384,448},{512,576},{640,704},{64,0},{1... | collective-permute-start | bytes 368648 | tf_op jit(solution)/shard_map/ppermute | solution.py:415
  17.6 2.5 %copy-start = (f32[5,5]{1,0:T(8,128)S(1)}, f32[5,5]{1,0:T(8,128)}, u32[]{:S(2)}) copy-start(f32[5,5]{1,0:T(8,128)} %mixing.3) | copy-start | bytes 304
  22.8 11.6 %collective-permute-start.4 = (f32[96,128]{1,0:T(8,128)S(1)}, f32[96,128]{1,0:T(8,128)S(1)}, u32[]{:S(2)}, u32[]{:S(2)}) collective-permute-start(f32[96,128]{1,0:T(8,128)S(1)} %get-tuple-element.37), channel_id=1, source_target_pairs={{2,4},{6,8},{10,12},{14,16},{18,20},{22,24},{26,28},{30,32},{34,36... | collective-permute-start | bytes 147464 | tf_op jit(solution)/shard_map/ppermute | solution.py:415
  27.9 6.6 %collective-permute-start.5 = (f32[96,128]{1,0:T(8,128)S(1)}, f32[96,128]{1,0:T(8,128)S(1)}, u32[]{:S(2)}, u32[]{:S(2)}) collective-permute-start(f32[96,128]{1,0:T(8,128)S(1)} %get-tuple-element.38), channel_id=1, source_target_pairs={{0,2},{4,6},{8,10},{12,14},{16,18},{20,22},{24,26},{28,30},{32,34}... | collective-permute-start | bytes 147464 | tf_op jit(solution)/shard_map/ppermute | solution.py:415
  34.5 8.8 %collective-permute-start.6 = (f32[96,128]{1,0:T(8,128)S(1)}, f32[96,128]{1,0:T(8,128)S(1)}, u32[]{:S(2)}, u32[]{:S(2)}) collective-permute-start(f32[96,128]{1,0:T(8,128)S(1)} %get-tuple-element.41), channel_id=1, source_target_pairs={{64,128},{192,256},{320,384},{448,512},{576,640},{128,64},{256,192... | collective-permute-start | bytes 147464 | tf_op jit(solution)/shard_map/ppermute | solution.py:415
  39.1 6.0 %collective-permute-start.7 = (f32[96,128]{1,0:T(8,128)S(1)}, f32[96,128]{1,0:T(8,128)S(1)}, u32[]{:S(2)}, u32[]{:S(2)}) collective-permute-start(f32[96,128]{1,0:T(8,128)S(1)} %get-tuple-element.42), channel_id=1, source_target_pairs={{0,64},{128,192},{256,320},{384,448},{512,576},{640,704},{64,0},{1... | collective-permute-start | bytes 147464 | tf_op jit(solution)/shard_map/ppermute | solution.py:415
